TPU v7x, 32 devices: a whole 2x2x4 slice. The times are simulated.
32 devices in a mesh: dp: 32 (over z, y, x, core).
Axes of the slice: x: 2, y: 2, z: 4, core: 2. Of those that a mesh axis runs over, the one named last changes fastest.
Arguments:
- tokens: bfloat16 [32768, 960], P('dp'), may hold values from -6 to 6
- position: int32 [32768], P('dp'), may hold values from -1 to 511, as said below
- cotangent: bfloat16 [32768, 960], P('dp'), may hold values from -6 to 6
- w_query: float32 [921600], P('dp'), may hold values from -0.1875 to 0.1875
- w_key: float32 [307200], P('dp'), may hold values from -0.1875 to 0.1875
- w_value: float32 [307200], P('dp'), may hold values from -0.1875 to 0.1875
- w_out: float32 [921600], P('dp'), may hold values from -1 to 1
- w_gate: float32 [2457600], P('dp'), may hold values from -0.1875 to 0.1875
- w_up: float32 [2457600], P('dp'), may hold values from -0.1875 to 0.1875
- w_down: float32 [2457600], P('dp'), may hold values from -0.125 to 0.125
- gain_attn: float32 [960], replicated, may hold values from 0.5 to 1.5
- gain_mlp: float32 [960], replicated, may hold values from 0.5 to 1.5
Outputs:
- output: bfloat16 [32768, 960], P('dp')
- grad_tokens: bfloat16 [32768, 960], P('dp')
- grad_w_query: float32 [921600], P('dp')
- grad_w_key: float32 [307200], P('dp')
- grad_w_value: float32 [307200], P('dp')
- grad_w_out: float32 [921600], P('dp')
- grad_w_gate: float32 [2457600], P('dp')
- grad_w_up: float32 [2457600], P('dp')
- grad_w_down: float32 [2457600], P('dp')
- grad_gain_attn: float32 [960], replicated
- grad_gain_mlp: float32 [960], replicated
Inputs may be any that keep to these rules, and one draw needn't show every extreme that they name: `position`: within each aligned block of 512 slots (one micro-batch): slot 0 holds 0; every other live slot holds 0 (a new sequence) or one more than the slot before it; empty slots (-1) come only after the last live slot; a quarter or more of the slots are live; in every draw one micro-batch holds a single sequence of 512 tokens.
All inputs are finite; a program needn't handle non-finite values.
Results may differ from a plain program's by a relative error of at most 0.012.
The roundings to bfloat16 on the way count: a program that leaves them out, or rounds other values in their place, can miss the bound.
Values may be sent and summed in bfloat16 or wider, within the bound.
A program may use at most 320 MiB of HBM per device.

v0:
```python
import math

import jax
import jax.numpy as jnp
from jax import lax
from jax.sharding import PartitionSpec as P

D = 960
H = 15
KV = 5
HD = 64
FF = 2560
SLOTS = 512


EPS = 1e-05
THETA = 100000.0


def block_mask(position):
    living = position >= 0
    placed = jnp.maximum(position, 0)
    sequence = jnp.cumsum((position == 0).astype(jnp.int32))
    allowed = (sequence[:, None] == sequence[None, :]) & (placed[None, :] <= placed[:, None])
    allowed = allowed & living[:, None] & living[None, :]
    slot_ids = jnp.arange(position.shape[0])
    return (allowed | (slot_ids[:, None] == slot_ids[None, :]), placed, living)


def rotary_tables(placed, head_size):
    half_ids = jnp.arange(head_size // 2, dtype=jnp.float32)
    freqs = THETA ** (-2.0 * half_ids / head_size)
    angles = placed.astype(jnp.float32)[:, None] * freqs[None, :]
    return (jnp.cos(angles)[:, None, :], jnp.sin(angles)[:, None, :])


def rotate(values, cosines, sines):
    half = values.shape[-1] // 2
    first_half = values[..., :half]
    second_half = values[..., half:]
    return jnp.concatenate(
        [first_half * cosines - second_half * sines, second_half * cosines + first_half * sines],
        axis=-1,
    )


def unrotate(grads, cosines, sines):
    half = grads.shape[-1] // 2
    first_half = grads[..., :half]
    second_half = grads[..., half:]
    return jnp.concatenate(
        [first_half * cosines + second_half * sines, second_half * cosines - first_half * sines],
        axis=-1,
    )


def matmul(first, second):
    return jnp.dot(first, second, preferred_element_type=jnp.float32)


def left_contract(first, second):
    return lax.dot_general(
        first, second, (((0,), (0,)), ((), ())), preferred_element_type=jnp.float32
    )


def right_contract(first, second):
    return lax.dot_general(
        first, second, (((1,), (1,)), ((), ())), preferred_element_type=jnp.float32
    )


def norm_back(grad_out, inputs, factor, gain):
    scaled = grad_out * gain
    return factor * scaled - inputs * factor * factor * factor * jnp.mean(
        scaled * inputs, axis=-1, keepdims=True
    )


def unfold(flat):
    kv_width = KV * HD
    return (
        flat[0].reshape(D, D),
        flat[1].reshape(D, kv_width),
        flat[2].reshape(D, kv_width),
        flat[3].reshape(D, D),
        flat[4].reshape(D, FF),
        flat[5].reshape(D, FF),
        flat[6].reshape(FF, D),
    )


def body(
    tokens,
    position,
    cotangent,
    w_query,
    w_key,
    w_value,
    w_out,
    w_gate,
    w_up,
    w_down,
    gain_attn,
    gain_mlp,
):
    slots = SLOTS
    groups = H // KV
    scale = 1.0 / math.sqrt(HD)
    shard_query = w_query.astype(jnp.bfloat16)
    shard_key = w_key.astype(jnp.bfloat16)
    shard_value = w_value.astype(jnp.bfloat16)
    shard_out = w_out.astype(jnp.bfloat16)
    shard_gate = w_gate.astype(jnp.bfloat16)
    shard_up = w_up.astype(jnp.bfloat16)
    shard_down = w_down.astype(jnp.bfloat16)
    blocks = tokens.shape[0] // slots
    items = (
        tokens.reshape(blocks, slots, D),
        position.reshape(blocks, slots),
        cotangent.reshape(blocks, slots, D),
    )

    def micro_step(totals, item):
        block_tokens, block_pos, block_cot = item
        front = unfold(
            (
                lax.all_gather(shard_query, "dp", axis=0, tiled=True),
                lax.all_gather(shard_key, "dp", axis=0, tiled=True),
                lax.all_gather(shard_value, "dp", axis=0, tiled=True),
                lax.all_gather(shard_out, "dp", axis=0, tiled=True),
                lax.all_gather(shard_gate, "dp", axis=0, tiled=True),
                lax.all_gather(shard_up, "dp", axis=0, tiled=True),
                lax.all_gather(shard_down, "dp", axis=0, tiled=True),
            )
        )
        allowed, placed, living = block_mask(block_pos)
        cosines, sines = rotary_tables(placed, HD)
        inputs = block_tokens.astype(jnp.float32)
        mat_query, mat_key, mat_value, mat_out, mat_gate, mat_up, mat_down = front
        factor_one = lax.rsqrt(jnp.mean(inputs * inputs, axis=-1, keepdims=True) + EPS)
        normed = (inputs * factor_one * gain_attn).astype(jnp.bfloat16)
        query = matmul(normed, mat_query).reshape(slots, H, HD)
        keys = matmul(normed, mat_key).reshape(slots, KV, HD)
        values = matmul(normed, mat_value).astype(jnp.bfloat16).reshape(slots, KV, HD)
        query_rot = (
            rotate(query, cosines, sines).astype(jnp.bfloat16).reshape(slots, KV, groups, HD)
        )
        keys_rot = rotate(keys, cosines, sines).astype(jnp.bfloat16)
        scores = (
            jnp.einsum("sgrd,tgd->grst", query_rot, keys_rot, preferred_element_type=jnp.float32)
            * scale
        )
        scores = jnp.where(allowed, scores, -1e30)
        top = jnp.max(scores, axis=-1, keepdims=True)
        expd = jnp.exp(scores - top)
        total_exp = jnp.sum(expd, axis=-1, keepdims=True)
        probs = expd / total_exp
        log_total = top + jnp.log(total_exp)
        mixed = jnp.einsum(
            "grst,tgd->sgrd", probs.astype(jnp.bfloat16), values, preferred_element_type=jnp.float32
        )
        mixed = mixed.reshape(slots, D).astype(jnp.bfloat16)
        resid = inputs + matmul(mixed, mat_out)
        factor_two = lax.rsqrt(jnp.mean(resid * resid, axis=-1, keepdims=True) + EPS)
        normed_two = (resid * factor_two * gain_mlp).astype(jnp.bfloat16)
        gate = matmul(normed_two, mat_gate)
        upper = matmul(normed_two, mat_up)
        sigma = jax.nn.sigmoid(gate)
        hidden = (gate * sigma * upper).astype(jnp.bfloat16)
        result = resid + matmul(hidden, mat_down)
        back = unfold(
            (
                lax.all_gather(shard_query, "dp", axis=0, tiled=True),
                lax.all_gather(shard_key, "dp", axis=0, tiled=True),
                lax.all_gather(shard_value, "dp", axis=0, tiled=True),
                lax.all_gather(shard_out, "dp", axis=0, tiled=True),
                lax.all_gather(shard_gate, "dp", axis=0, tiled=True),
                lax.all_gather(shard_up, "dp", axis=0, tiled=True),
                lax.all_gather(shard_down, "dp", axis=0, tiled=True),
            )
        )
        bq_mat, bk_mat, bv_mat, bo_mat, bg_mat, bu_mat, bd_mat = back
        grad_out = block_cot.astype(jnp.float32) * living[:, None].astype(jnp.float32)
        grad_out_b = grad_out.astype(jnp.bfloat16)
        grad_down = left_contract(hidden, grad_out_b)
        d_hidden = right_contract(grad_out_b, bd_mat)
        d_upper = (d_hidden * gate * sigma).astype(jnp.bfloat16)
        d_gate = (d_hidden * upper * sigma * (1.0 + gate * (1.0 - sigma))).astype(jnp.bfloat16)
        grad_gate = left_contract(normed_two, d_gate)
        grad_up = left_contract(normed_two, d_upper)
        d_normed_two = right_contract(d_gate, bg_mat) + right_contract(d_upper, bu_mat)
        gain_two_grad = jnp.sum(d_normed_two * resid * factor_two, axis=0)
        d_resid = grad_out + norm_back(d_normed_two, resid, factor_two, gain_mlp)
        d_attn = d_resid.astype(jnp.bfloat16)
        grad_wout = left_contract(mixed, d_attn)
        d_mixed = right_contract(d_attn, bo_mat).astype(jnp.bfloat16).reshape(slots, KV, groups, HD)
        d_probs = jnp.einsum("sgrd,tgd->grst", d_mixed, values, preferred_element_type=jnp.float32)
        scores_back = (
            jnp.einsum("sgrd,tgd->grst", query_rot, keys_rot, preferred_element_type=jnp.float32)
            * scale
        )
        scores_back = jnp.where(allowed, scores_back, -1e30)
        probs_back = jnp.exp(scores_back - log_total)
        d_values = jnp.einsum(
            "grst,sgrd->tgd",
            probs_back.astype(jnp.bfloat16),
            d_mixed,
            preferred_element_type=jnp.float32,
        )
        d_values = d_values.reshape(slots, KV * HD).astype(jnp.bfloat16)
        d_scores = probs_back * (d_probs - jnp.sum(probs_back * d_probs, axis=-1, keepdims=True))
        d_scores = d_scores.astype(jnp.bfloat16)
        d_query_rot = (
            jnp.einsum("grst,tgd->sgrd", d_scores, keys_rot, preferred_element_type=jnp.float32)
            * scale
        )
        d_keys_rot = (
            jnp.einsum("grst,sgrd->tgd", d_scores, query_rot, preferred_element_type=jnp.float32)
            * scale
        )
        d_query = (
            unrotate(d_query_rot.reshape(slots, H, HD), cosines, sines)
            .reshape(slots, D)
            .astype(jnp.bfloat16)
        )
        d_keys = unrotate(d_keys_rot, cosines, sines).reshape(slots, KV * HD).astype(jnp.bfloat16)
        grad_query = left_contract(normed, d_query)
        grad_key = left_contract(normed, d_keys)
        grad_value = left_contract(normed, d_values)
        d_normed = (
            right_contract(d_query, bq_mat)
            + right_contract(d_keys, bk_mat)
            + right_contract(d_values, bv_mat)
        )
        gain_one_grad = jnp.sum(d_normed * inputs * factor_one, axis=0)
        d_inputs = d_resid + norm_back(d_normed, inputs, factor_one, gain_attn)
        new_totals = (
            totals[0] + grad_query,
            totals[1] + grad_key,
            totals[2] + grad_value,
            totals[3] + grad_wout,
            totals[4] + grad_gate,
            totals[5] + grad_up,
            totals[6] + grad_down,
            totals[7] + gain_one_grad,
            totals[8] + gain_two_grad,
        )
        return (new_totals, (result.astype(jnp.bfloat16), d_inputs.astype(jnp.bfloat16)))

    start = (
        jnp.zeros((D, D), jnp.float32),
        jnp.zeros((D, KV * HD), jnp.float32),
        jnp.zeros((D, KV * HD), jnp.float32),
        jnp.zeros((D, D), jnp.float32),
        jnp.zeros((D, FF), jnp.float32),
        jnp.zeros((D, FF), jnp.float32),
        jnp.zeros((FF, D), jnp.float32),
        jnp.zeros((D,), jnp.float32),
        jnp.zeros((D,), jnp.float32),
    )
    totals, (results, input_grads) = lax.scan(micro_step, start, items)
    owners = lax.axis_size("dp")
    members = [totals[index].reshape(owners, -1) for index in range(7)]
    widths = [member.shape[1] for member in members]
    stacked = jnp.concatenate(members, axis=1)
    summed_row = lax.psum_scatter(stacked, "dp", scatter_dimension=0, tiled=True).reshape(-1)
    pieces = []
    offset = 0
    for width in widths:
        pieces.append(summed_row[offset : offset + width])
        offset = offset + width
    gains = lax.psum((totals[7], totals[8]), "dp")
    return (
        results.reshape(blocks * slots, D),
        input_grads.reshape(blocks * slots, D),
        pieces[0],
        pieces[1],
        pieces[2],
        pieces[3],
        pieces[4],
        pieces[5],
        pieces[6],
        gains[0],
        gains[1],
    )


def solution(mesh):
    placed = (
        P("dp", None),
        P("dp"),
        P("dp", None),
        P("dp"),
        P("dp"),
        P("dp"),
        P("dp"),
        P("dp"),
        P("dp"),
        P("dp"),
        P(),
        P(),
    )
    return jax.shard_map(
        body,
        mesh=mesh,
        in_specs=placed,
        out_specs=(
            P("dp", None),
            P("dp", None),
            P("dp"),
            P("dp"),
            P("dp"),
            P("dp"),
            P("dp"),
            P("dp"),
            P("dp"),
            P(),
            P(),
        ),
        check_vma=False,
    )
```

profile of v0, /device:TPU:0, one launch (start us, length us, event | category | flops | bytes accessed | tf_op | source)
XLA Modules:
  0.0 1577.5 jit_solution(11332907884921091458)
XLA Ops:
  19.6 879.6 %while.33 = (s32[]{:T(128)}, f32[960,960]{1,0:T(8,128)}, f32[960,320]{0,1:T(8,128)}, f32[960,320]{0,1:T(8,128)}, f32[960,960]{1,0:T(8,128)}, /*index=5*/f32[960,...) while((s32[]{:T(128)}, f32[960,960]{1,0:T(8,128)}, ...), condition=%wide.region_12.13_spmd.clone, body=%wide.region_0.12_spmd.clone.sunk | while | flops 33382666240 | bytes 1089391488 | solution.py:262
  25.2 48.2 %all-gather.13 = bf16[32,1,9600]{2,1,0:T(2,128)(2,1)S(1)} all-gather(bf16[1,1,9600]{2,1,0:T(2,128)(2,1)S(1)} %reshape.580), channel_id=1, replica_groups=mesh['dp'=32] {'dp'}, dimensions={0}, use_global_device_ids=true | all-gather | bytes 633600 | tf_op jit(solution)/shard_map/while/body/eval_jaxpr/all_gather | solution.py:129
  81.0 43.8 %all-gather.14 = bf16[32,1,9600]{2,1,0:T(2,128)(2,1)} all-gather(bf16[1,1,9600]{2,1,0:T(2,128)(2,1)S(1)} %reshape.582), channel_id=1, replica_groups=mesh['dp'=32] {'dp'}, dimensions={0}, use_global_device_ids=true | all-gather | bytes 633600 | tf_op jit(solution)/shard_map/while/body/eval_jaxpr/all_gather | solution.py:130
  137.3 41.2 %reduce.24 = bf16[32,28800]{1,0:T(8,128)(2,1)} reduce(bf16[32,1,28800]{2,1,0:T(2,128)(2,1)} %all-gather.22.cloned.1.call-done, bf16[]{:T(256)} %constant.226..sunk), dimensions={1}, to_apply=%all-gather.5.reduce_sub_computation | reduce | bytes 3686402 | tf_op jit(solution)/shard_map/while/body/eval_jaxpr/all_gather | solution.py:128
  182.5 40.8 %reduce.27 = bf16[32,28800]{1,0:T(8,128)(2,1)} reduce(bf16[32,1,28800]{2,1,0:T(2,128)(2,1)} %all-gather.24.cloned.1.call-done, bf16[]{:T(256)} %constant.226..sunk), dimensions={1}, to_apply=%all-gather.7.reduce_sub_computation | reduce | bytes 3686402 | tf_op jit(solution)/shard_map/while/body/eval_jaxpr/all_gather | solution.py:131
  260.2 10.0 reshape.586
  270.2 15.6 all-gather.28.cloned.1.call-done
  285.8 9.6 reshape.587
  295.4 8.2 fusion.243
  308.6 43.2 %all-gather.30.cloned.1.call-done = bf16[2457600]{0:T(1024)(128)(2,1)} async-done(((bf16[76800]{0:T(1024)(128)(2,1)}), bf16[2457600]{0:T(1024)(128)(2,1)}) %all-gather.30.cloned.1.call-update) | async-done | bytes 4915216 | tf_op jit(solution)/shard_map/while/body/eval_jaxpr/all_gather | solution.py:133
  351.8 10.1 reshape.588
  361.9 10.5 multiply_convert_fusion.7
  424.1 8.3 select_add_fusion.16
  463.6 43.9 %all-gather.13 = bf16[32,1,9600]{2,1,0:T(2,128)(2,1)S(1)} all-gather(bf16[1,1,9600]{2,1,0:T(2,128)(2,1)S(1)} %reshape.580), channel_id=1, replica_groups=mesh['dp'=32] {'dp'}, dimensions={0}, use_global_device_ids=true | all-gather | bytes 633600 | tf_op jit(solution)/shard_map/while/body/eval_jaxpr/all_gather | solution.py:129
  515.0 44.0 %all-gather.14 = bf16[32,1,9600]{2,1,0:T(2,128)(2,1)} all-gather(bf16[1,1,9600]{2,1,0:T(2,128)(2,1)S(1)} %reshape.582), channel_id=1, replica_groups=mesh['dp'=32] {'dp'}, dimensions={0}, use_global_device_ids=true | all-gather | bytes 633600 | tf_op jit(solution)/shard_map/while/body/eval_jaxpr/all_gather | solution.py:130
  571.6 41.2 %reduce.24 = bf16[32,28800]{1,0:T(8,128)(2,1)} reduce(bf16[32,1,28800]{2,1,0:T(2,128)(2,1)} %all-gather.22.cloned.1.call-done, bf16[]{:T(256)} %constant.226..sunk), dimensions={1}, to_apply=%all-gather.5.reduce_sub_computation | reduce | bytes 3686402 | tf_op jit(solution)/shard_map/while/body/eval_jaxpr/all_gather | solution.py:128
  617.0 40.8 %reduce.27 = bf16[32,28800]{1,0:T(8,128)(2,1)} reduce(bf16[32,1,28800]{2,1,0:T(2,128)(2,1)} %all-gather.24.cloned.1.call-done, bf16[]{:T(256)} %constant.226..sunk), dimensions={1}, to_apply=%all-gather.7.reduce_sub_computation | reduce | bytes 3686402 | tf_op jit(solution)/shard_map/while/body/eval_jaxpr/all_gather | solution.py:131
  694.7 10.0 reshape.586
  704.7 14.0 all-gather.28.cloned.1.call-done
  718.7 9.6 reshape.587
  728.3 8.2 fusion.243
  741.4 43.2 %all-gather.30.cloned.1.call-done = bf16[2457600]{0:T(1024)(128)(2,1)} async-done(((bf16[76800]{0:T(1024)(128)(2,1)}), bf16[2457600]{0:T(1024)(128)(2,1)}) %all-gather.30.cloned.1.call-update) | async-done | bytes 4915216 | tf_op jit(solution)/shard_map/while/body/eval_jaxpr/all_gather | solution.py:133
  784.7 10.1 reshape.588
  794.7 10.5 multiply_convert_fusion.7
  856.9 8.3 select_add_fusion.16
  914.2 10.3 reshape.516
  924.5 10.3 reshape.517
  934.9 11.2 copy.54
  946.0 10.6 reshape.518
  966.0 8.6 constant_dynamic-update-slice_fusion.2
  992.6 41.8 %all-reduce.1 = (f32[960]{0:T(1024)}, f32[960]{0:T(1024)}) all-reduce(f32[960]{0:T(1024)S(1)} %copy-done.77, f32[960]{0:T(1024)S(1)} %copy-done.74), channel_id=1, replica_groups=mesh['dp'=32] {'dp'}, use_global_device_ids=true, to_apply=%region_14.15 | all-reduce | flops 1920 | bytes 15360 | tf_op jit(solution)/shard_map/psum | solution.py:273
  1034.4 524.5 %all-reduce.4.cloned.1.call-done = f32[32,307200]{1,0:T(8,128)} async-done(((f32[32,307200]{1,0:T(8,128)}), f32[32,307200]{1,0:T(8,128)}) %all-reduce.4.cloned.1.call-update) | async-done | bytes 39321616
  (588 shorter events, 359.2 us)
Async XLA Ops:
  19.6 58.3 %copy-start.67 = (bf16[9600]{0:T(1024)(128)(2,1)}, bf16[9600]{0:T(1024)(128)(2,1)S(1)}, u32[]{:S(2)}) copy-start(bf16[9600]{0:T(1024)(128)(2,1)S(1)} %get-tuple-element.807) | copy-start | bytes 57604 | tf_op jit(solution)/shard_map/while
  19.6 58.3 %copy-start.69 = (bf16[9600]{0:T(1024)(128)(2,1)}, bf16[9600]{0:T(1024)(128)(2,1)S(1)}, u32[]{:S(2)}) copy-start(bf16[9600]{0:T(1024)(128)(2,1)S(1)} %get-tuple-element.810) | copy-start | bytes 57604 | tf_op jit(solution)/shard_map/while
  19.6 237.6 %copy-start.3 = (bf16[2,512,960]{1,2,0:T(8,128)(2,1)}, bf16[2,512,960]{1,2,0:T(8,128)(2,1)S(1)}, u32[]{:S(2)}) copy-start(bf16[2,512,960]{1,2,0:T(8,128)(2,1)S(1)} %get-tuple-element.805) | copy-start | bytes 5898244 | tf_op jit(solution)/shard_map/while
  19.7 117.6 %all-gather.22.cloned.1.call-start = ((), (), s32[]{:S(2)}) async-start(), calls=%async_computation.1 | async-start | bytes 3801600 | tf_op jit(solution)/shard_map/while/body/eval_jaxpr/all_gather | solution.py:128
  20.7 161.8 %all-gather.24.cloned.1.call-start = ((), (), s32[]{:S(2)}) async-start(), calls=%async_computation.2 | async-start | bytes 3801600 | tf_op jit(solution)/shard_map/while/body/eval_jaxpr/all_gather | solution.py:131
  21.4 238.8 %all-gather.26.cloned.1.call-start = ((), (), s32[]{:S(2)}) async-start(), calls=%async_computation.3 | async-start | bytes 5068800 | tf_op jit(solution)/shard_map/while/body/eval_jaxpr/all_gather | solution.py:132
  22.2 263.6 %all-gather.28.cloned.1.call-start = ((), (), s32[]{:S(2)}) async-start(), calls=%async_computation.4 | async-start | bytes 5068800 | tf_op jit(solution)/shard_map/while/body/eval_jaxpr/all_gather | solution.py:180
  22.8 329.0 %all-gather.30.cloned.1.call-start = ((), (), s32[]{:S(2)}) async-start(), calls=%async_computation.5 | async-start | bytes 5068800 | tf_op jit(solution)/shard_map/while/body/eval_jaxpr/all_gather | solution.py:133
  79.8 50.5 %copy-start.12 = (bf16[960,320]{1,0:T(8,128)(2,1)}, bf16[960,320]{1,0:T(8,128)(2,1)S(1)}, u32[]{:S(2)}) copy-start(bf16[960,320]{1,0:T(8,128)(2,1)S(1)} %reshape.581) | copy-start | bytes 1843204 | tf_op jit(solution)/shard_map/while
  132.6 98.5 %copy-start.65 = (f32[512]{0:T(512)}, f32[512]{0:T(512)S(1)}, u32[]{:S(2)}) copy-start(f32[512]{0:T(512)S(1)} %add_rsqrt_fusion.4) | copy-start | bytes 6148 | tf_op jit(solution)/shard_map/while
  133.0 100.9 %copy-start.35 = (f32[512,32]{0,1:T(8,128)}, f32[512,32]{0,1:T(8,128)S(1)}, u32[]{:S(2)}) copy-start(f32[512,32]{0,1:T(8,128)S(1)} %get-tuple-element.711) | copy-start | bytes 196612 | tf_op jit(solution)/shard_map/while
  133.0 100.9 %copy-start.37 = (f32[512,32]{0,1:T(8,128)}, f32[512,32]{0,1:T(8,128)S(1)}, u32[]{:S(2)}) copy-start(f32[512,32]{0,1:T(8,128)S(1)} %get-tuple-element.710) | copy-start | bytes 196612 | tf_op jit(solution)/shard_map/while
  136.6 97.8 %copy-start.43 = (bf16[512,5,32]{0,2,1:T(8,128)(2,1)}, bf16[512,5,32]{0,2,1:T(8,128)(2,1)S(1)}, u32[]{:S(2)}) copy-start(bf16[512,5,32]{0,2,1:T(8,128)(2,1)S(1)} %get-tuple-element.715) | copy-start | bytes 491524 | tf_op jit(solution)/shard_map/while
  137.3 112.7 %copy-start.41 = (bf16[512,320]{0,1:T(8,128)(2,1)}, bf16[512,320]{0,1:T(8,128)(2,1)S(1)}, u32[]{:S(2)}) copy-start(bf16[512,320]{0,1:T(8,128)(2,1)S(1)} %convolution_convert_fusion.4) | copy-start | bytes 983044 | tf_op jit(solution)/shard_map/while
  382.7 31.3 %copy-start.5 = (f32[512,960]{0,1:T(8,128)}, f32[512,960]{0,1:T(8,128)S(1)}, u32[]{:S(2)}) copy-start(f32[512,960]{0,1:T(8,128)S(1)} %fusion.245) | copy-start | bytes 5898244 | tf_op jit(solution)/shard_map/while
  457.8 54.2 %copy-start.67 = (bf16[9600]{0:T(1024)(128)(2,1)}, bf16[9600]{0:T(1024)(128)(2,1)S(1)}, u32[]{:S(2)}) copy-start(bf16[9600]{0:T(1024)(128)(2,1)S(1)} %get-tuple-element.807) | copy-start | bytes 57604 | tf_op jit(solution)/shard_map/while
  457.8 54.1 %copy-start.69 = (bf16[9600]{0:T(1024)(128)(2,1)}, bf16[9600]{0:T(1024)(128)(2,1)S(1)}, u32[]{:S(2)}) copy-start(bf16[9600]{0:T(1024)(128)(2,1)S(1)} %get-tuple-element.810) | copy-start | bytes 57604 | tf_op jit(solution)/shard_map/while
  457.9 233.9 %copy-start.3 = (bf16[2,512,960]{1,2,0:T(8,128)(2,1)}, bf16[2,512,960]{1,2,0:T(8,128)(2,1)S(1)}, u32[]{:S(2)}) copy-start(bf16[2,512,960]{1,2,0:T(8,128)(2,1)S(1)} %get-tuple-element.805) | copy-start | bytes 5898244 | tf_op jit(solution)/shard_map/while
  457.9 113.8 %all-gather.22.cloned.1.call-start = ((), (), s32[]{:S(2)}) async-start(), calls=%async_computation.1 | async-start | bytes 3801600 | tf_op jit(solution)/shard_map/while/body/eval_jaxpr/all_gather | solution.py:128
  458.9 158.1 %all-gather.24.cloned.1.call-start = ((), (), s32[]{:S(2)}) async-start(), calls=%async_computation.2 | async-start | bytes 3801600 | tf_op jit(solution)/shard_map/while/body/eval_jaxpr/all_gather | solution.py:131
  459.7 235.0 %all-gather.26.cloned.1.call-start = ((), (), s32[]{:S(2)}) async-start(), calls=%async_computation.3 | async-start | bytes 5068800 | tf_op jit(solution)/shard_map/while/body/eval_jaxpr/all_gather | solution.py:132
  460.4 258.3 %all-gather.28.cloned.1.call-start = ((), (), s32[]{:S(2)}) async-start(), calls=%async_computation.4 | async-start | bytes 5068800 | tf_op jit(solution)/shard_map/while/body/eval_jaxpr/all_gather | solution.py:180
  461.1 323.5 %all-gather.30.cloned.1.call-start = ((), (), s32[]{:S(2)}) async-start(), calls=%async_computation.5 | async-start | bytes 5068800 | tf_op jit(solution)/shard_map/while/body/eval_jaxpr/all_gather | solution.py:133
  513.9 50.7 %copy-start.12 = (bf16[960,320]{1,0:T(8,128)(2,1)}, bf16[960,320]{1,0:T(8,128)(2,1)S(1)}, u32[]{:S(2)}) copy-start(bf16[960,320]{1,0:T(8,128)(2,1)S(1)} %reshape.581) | copy-start | bytes 1843204 | tf_op jit(solution)/shard_map/while
  566.9 98.7 %copy-start.65 = (f32[512]{0:T(512)}, f32[512]{0:T(512)S(1)}, u32[]{:S(2)}) copy-start(f32[512]{0:T(512)S(1)} %add_rsqrt_fusion.4) | copy-start | bytes 6148 | tf_op jit(solution)/shard_map/while
  567.3 101.1 %copy-start.35 = (f32[512,32]{0,1:T(8,128)}, f32[512,32]{0,1:T(8,128)S(1)}, u32[]{:S(2)}) copy-start(f32[512,32]{0,1:T(8,128)S(1)} %get-tuple-element.711) | copy-start | bytes 196612 | tf_op jit(solution)/shard_map/while
  567.3 101.1 %copy-start.37 = (f32[512,32]{0,1:T(8,128)}, f32[512,32]{0,1:T(8,128)S(1)}, u32[]{:S(2)}) copy-start(f32[512,32]{0,1:T(8,128)S(1)} %get-tuple-element.710) | copy-start | bytes 196612 | tf_op jit(solution)/shard_map/while
  570.9 97.9 %copy-start.43 = (bf16[512,5,32]{0,2,1:T(8,128)(2,1)}, bf16[512,5,32]{0,2,1:T(8,128)(2,1)S(1)}, u32[]{:S(2)}) copy-start(bf16[512,5,32]{0,2,1:T(8,128)(2,1)S(1)} %get-tuple-element.715) | copy-start | bytes 491524 | tf_op jit(solution)/shard_map/while
  571.6 112.8 %copy-start.41 = (bf16[512,320]{0,1:T(8,128)(2,1)}, bf16[512,320]{0,1:T(8,128)(2,1)S(1)}, u32[]{:S(2)}) copy-start(bf16[512,320]{0,1:T(8,128)(2,1)S(1)} %convolution_convert_fusion.4) | copy-start | bytes 983044 | tf_op jit(solution)/shard_map/while
  784.7 20.6 %slice-start.15 = ((s8[4915200]{0:T(1024)(128)(4,1)}), s8[720896]{0:T(1024)(128)(4,1)S(1)}, s32[]{:S(2)}) async-start(s8[4915200]{0:T(1024)(128)(4,1)} %bitcast.341), calls=%async_computation.21 | async-start | bytes 1441792 | tf_op jit(solution)/shard_map/while
  815.5 31.3 %copy-start.5 = (f32[512,960]{0,1:T(8,128)}, f32[512,960]{0,1:T(8,128)S(1)}, u32[]{:S(2)}) copy-start(f32[512,960]{0,1:T(8,128)S(1)} %fusion.245) | copy-start | bytes 5898244 | tf_op jit(solution)/shard_map/while
  899.2 659.7 %all-reduce.4.cloned.1.call-start = ((), (), s32[]{:S(2)}) async-start(), calls=%async_computation | async-start | bytes 78643200
  (167 other events, 764.8 us)
Sparse Core Ops, SparseCore 0:
  23.9 66.3 all-gather.21
  93.7 59.8 all-gather.23
  156.6 63.2 all-gather.25
  222.7 63.1 all-gather.27
  288.6 63.1 all-gather.29
  461.8 61.5 all-gather.21
  526.8 59.4 all-gather.23
  589.3 63.2 all-gather.25
  655.5 63.1 all-gather.27
  721.4 63.1 all-gather.29
Sparse Core Ops, SparseCore 1:
  987.3 571.6 all-reduce.3
where the time goes:
time: 1580 us
  waiting for transfers between devices  644 us (41%)
  local copies, waits for them, and re-layouts  243 us (15%)
  other arithmetic  236 us (15%)
  blocking collectives  222 us (14%)
  matrix products  205 us (13%)
  between operations  16 us (1%)
    unnamed x2, waiting for transfers between devices  524 us
    all_gather x2, blocking collectives, micro_step(): lax.all_gather(shard_key, 'dp', axis=0, tiled=True)  92.1 us
    all_gather x2, blocking collectives, micro_step(): lax.all_gather(shard_value, 'dp', axis=0, tiled=True)  87.9 us
    all_gather x2, waiting for transfers between devices, micro_step(): lax.all_gather(shard_up, 'dp', axis=0, tiled=True)  86.4 us
    all_gather x2, other arithmetic, micro_step(): lax.all_gather(shard_query, 'dp', axis=0, tiled=True)  82.5 us
    all_gather x2, other arithmetic, micro_step(): lax.all_gather(shard_out, 'dp', axis=0, tiled=True)  81.6 us
    dot_general x14, matrix products, left_contract(): lax.dot_general(first, second, (((0,), (0,)), ((), ())), preferred_elemen...  55.7 us
    dot_general x14, matrix products, matmul(): return jnp.dot(first, second, preferred_element_type=jnp.float32)  51.1 us
  transfers between devices with their start and end apart: 11, of which 5 were waited for; matrix products, arithmetic and copies ran while one was open for 23% of the time, Pallas kernels for 0%

commit v1 on v0

v1 whole, which is shorter than its diff:
```python
import math

import jax
import jax.numpy as jnp
from jax import lax
from jax.sharding import PartitionSpec as P

D = 960
H = 15
KV = 5
HD = 64
FF = 2560
SLOTS = 512


EPS = 1e-05
THETA = 100000.0


def block_mask(position):
    living = position >= 0
    placed = jnp.maximum(position, 0)
    sequence = jnp.cumsum((position == 0).astype(jnp.int32))
    allowed = (sequence[:, None] == sequence[None, :]) & (placed[None, :] <= placed[:, None])
    allowed = allowed & living[:, None] & living[None, :]
    slot_ids = jnp.arange(position.shape[0])
    return (allowed | (slot_ids[:, None] == slot_ids[None, :]), placed, living)


def rotary_tables(placed, head_size):
    half_ids = jnp.arange(head_size // 2, dtype=jnp.float32)
    freqs = THETA ** (-2.0 * half_ids / head_size)
    angles = placed.astype(jnp.float32)[:, None] * freqs[None, :]
    return (jnp.cos(angles)[:, None, :], jnp.sin(angles)[:, None, :])


def rotate(values, cosines, sines):
    half = values.shape[-1] // 2
    first_half = values[..., :half]
    second_half = values[..., half:]
    return jnp.concatenate(
        [first_half * cosines - second_half * sines, second_half * cosines + first_half * sines],
        axis=-1,
    )


def unrotate(grads, cosines, sines):
    half = grads.shape[-1] // 2
    first_half = grads[..., :half]
    second_half = grads[..., half:]
    return jnp.concatenate(
        [first_half * cosines + second_half * sines, second_half * cosines - first_half * sines],
        axis=-1,
    )


def matmul(first, second):
    return jnp.dot(first, second, preferred_element_type=jnp.float32)


def left_contract(first, second):
    return lax.dot_general(
        first, second, (((0,), (0,)), ((), ())), preferred_element_type=jnp.float32
    )


def right_contract(first, second):
    return lax.dot_general(
        first, second, (((1,), (1,)), ((), ())), preferred_element_type=jnp.float32
    )


def norm_back(grad_out, inputs, factor, gain):
    scaled = grad_out * gain
    return factor * scaled - inputs * factor * factor * factor * jnp.mean(
        scaled * inputs, axis=-1, keepdims=True
    )


def swap(value, bit):
    owners = lax.axis_size("dp")
    return lax.ppermute(value, "dp", [(i, i ^ (1 << bit)) for i in range(owners)])


def my_bit(bit):
    return (lax.axis_index("dp") >> bit) & 1


def gather_rows(shard, order):
    current = shard[None]
    held = []
    for bit in order:
        other = swap(current, bit)
        place = sum(1 for b in held if b > bit)
        shape = current.shape
        split = (1 << place, 1, shape[0] >> place) + shape[1:]
        mine, theirs = current.reshape(split), other.reshape(split)
        upper = my_bit(bit) == 1
        low = jnp.where(upper, theirs, mine)
        high = jnp.where(upper, mine, theirs)
        current = jnp.concatenate([low, high], axis=1).reshape((shape[0] * 2,) + shape[1:])
        held.append(bit)
    return current


def scatter_rows(parts, order):
    current = parts
    left = list(range(len(order)))
    for step, bit in enumerate(order):
        place = sum(1 for b in left if b > bit)
        shape = current.shape
        split = (1 << place, 2, shape[0] >> (place + 1)) + shape[1:]
        view = current.reshape(split)
        mine = my_bit(bit)
        sent = lax.dynamic_index_in_dim(view, 1 - mine, 1, keepdims=False)
        kept = lax.dynamic_index_in_dim(view, mine, 1, keepdims=False)
        got = swap(sent, bit)
        total = kept.astype(jnp.float32) + got.astype(jnp.float32)
        if step < len(order) - 1:
            total = total.astype(jnp.bfloat16)
        current = total.reshape((shape[0] // 2,) + shape[1:])
        left.remove(bit)
    return current[0]


def total_over(value, order):
    for bit in order:
        value = value + swap(value, bit)
    return value


def orders():
    bits = max(lax.axis_size("dp").bit_length() - 1, 0)
    far = list(range(3, bits))
    near_x = [bit for bit in (1, 2) if bit < bits]
    core = [0] if bits else []
    return core, near_x, far


def gather_order(flip):
    core, near, far = orders()
    return far + (near[::-1] if flip else near) + core


def scatter_order(flip):
    core, near, far = orders()
    return core + (near[::-1] if flip else near) + far[::-1]


def whole_rows(flat, width):
    return flat.shape[0] % width == 0


def gather_matrix(flat, width, flip):
    shard = flat.astype(jnp.bfloat16)
    if whole_rows(flat, width):
        shard = flat.reshape(-1, width).astype(jnp.bfloat16)
    return gather_rows(shard, gather_order(flip)).reshape(-1, width)


def scatter_matrix(grad, flip):
    owners = lax.axis_size("dp")
    grad = grad.astype(jnp.bfloat16)
    if grad.shape[0] % owners == 0:
        parts = grad.reshape(owners, grad.shape[0] // owners, grad.shape[1])
    else:
        parts = grad.reshape(owners, -1)
    return scatter_rows(parts, scatter_order(flip))


def attend(query_rot, keys_rot, values, allowed, scale):
    scores = (
        jnp.einsum("bsgrd,btgd->bgrst", query_rot, keys_rot, preferred_element_type=jnp.float32)
        * scale
    )
    return jnp.where(allowed[:, None, None], scores, -1e30)


def body(
    tokens,
    position,
    cotangent,
    w_query,
    w_key,
    w_value,
    w_out,
    w_gate,
    w_up,
    w_down,
    gain_attn,
    gain_mlp,
):
    slots = SLOTS
    groups = H // KV
    kvw = KV * HD
    scale = 1.0 / math.sqrt(HD)
    rows = tokens.shape[0]
    blocks = rows // slots
    if whole_rows(w_query, D):
        joined = jnp.concatenate(
            [
                w_query.reshape(-1, D),
                w_key.reshape(-1, kvw),
                w_value.reshape(-1, kvw),
                w_out.reshape(-1, D),
            ],
            axis=1,
        ).astype(jnp.bfloat16)
        joined = gather_rows(joined, gather_order(False)).reshape(D, D + 2 * kvw + D)
        mat_qkv = joined[:, : D + 2 * kvw]
        mat_out = joined[:, D + 2 * kvw :]
    else:
        mat_qkv = jnp.concatenate(
            [
                gather_matrix(w_query, D, False),
                gather_matrix(w_key, kvw, False),
                gather_matrix(w_value, kvw, False),
            ],
            axis=1,
        )
        mat_out = gather_matrix(w_out, D, False)
    mat_gate = gather_matrix(w_gate, FF, True)
    mat_up = gather_matrix(w_up, FF, False)
    mat_down = gather_matrix(w_down, D, True)

    allowed, placed, living = jax.vmap(block_mask)(position.reshape(blocks, slots))
    cosines, sines = rotary_tables(placed.reshape(-1), HD)
    living = living.reshape(-1)
    inputs = tokens.astype(jnp.float32)
    factor_one = lax.rsqrt(jnp.mean(inputs * inputs, axis=-1, keepdims=True) + EPS)
    normed = (inputs * factor_one * gain_attn).astype(jnp.bfloat16)
    qkv = matmul(normed, mat_qkv)
    query = qkv[:, :D].reshape(rows, H, HD)
    keys = qkv[:, D : D + kvw].reshape(rows, KV, HD)
    values = qkv[:, D + kvw :].astype(jnp.bfloat16).reshape(blocks, slots, KV, HD)
    query_rot = (
        rotate(query, cosines, sines).astype(jnp.bfloat16).reshape(blocks, slots, KV, groups, HD)
    )
    keys_rot = rotate(keys, cosines, sines).astype(jnp.bfloat16).reshape(blocks, slots, KV, HD)
    scores = attend(query_rot, keys_rot, values, allowed, scale)
    top = jnp.max(scores, axis=-1, keepdims=True)
    expd = jnp.exp(scores - top)
    total_exp = jnp.sum(expd, axis=-1, keepdims=True)
    probs = (expd / total_exp).astype(jnp.bfloat16)
    mixed = jnp.einsum("bgrst,btgd->bsgrd", probs, values, preferred_element_type=jnp.float32)
    mixed = mixed.reshape(rows, D).astype(jnp.bfloat16)
    resid = inputs + matmul(mixed, mat_out)
    factor_two = lax.rsqrt(jnp.mean(resid * resid, axis=-1, keepdims=True) + EPS)
    normed_two = (resid * factor_two * gain_mlp).astype(jnp.bfloat16)
    gate = matmul(normed_two, mat_gate)
    upper = matmul(normed_two, mat_up)
    sigma = jax.nn.sigmoid(gate)
    hidden = (gate * sigma * upper).astype(jnp.bfloat16)
    result = (resid + matmul(hidden, mat_down)).astype(jnp.bfloat16)

    grad_out = cotangent.astype(jnp.float32) * living[:, None].astype(jnp.float32)
    grad_out_b = grad_out.astype(jnp.bfloat16)
    sum_down = scatter_matrix(left_contract(hidden, grad_out_b), False)
    d_hidden = right_contract(grad_out_b, mat_down)
    d_upper = (d_hidden * gate * sigma).astype(jnp.bfloat16)
    d_gate = (d_hidden * upper * sigma * (1.0 + gate * (1.0 - sigma))).astype(jnp.bfloat16)
    sum_gate = scatter_matrix(left_contract(normed_two, d_gate), True)
    sum_up = scatter_matrix(left_contract(normed_two, d_upper), False)
    d_normed_two = right_contract(d_gate, mat_gate) + right_contract(d_upper, mat_up)
    gain_two = jnp.sum(d_normed_two * resid * factor_two, axis=0)
    d_resid = grad_out + norm_back(d_normed_two, resid, factor_two, gain_mlp)
    d_attn = d_resid.astype(jnp.bfloat16)
    sum_wout = scatter_matrix(left_contract(mixed, d_attn), True)
    d_mixed = right_contract(d_attn, mat_out).astype(jnp.bfloat16)
    d_mixed = d_mixed.reshape(blocks, slots, KV, groups, HD)
    d_probs = jnp.einsum("bsgrd,btgd->bgrst", d_mixed, values, preferred_element_type=jnp.float32)
    probs_back = expd / total_exp
    d_values = jnp.einsum("bgrst,bsgrd->btgd", probs, d_mixed, preferred_element_type=jnp.float32)
    d_values = d_values.reshape(rows, kvw).astype(jnp.bfloat16)
    d_scores = probs_back * (d_probs - jnp.sum(probs_back * d_probs, axis=-1, keepdims=True))
    d_scores = d_scores.astype(jnp.bfloat16)
    d_query_rot = (
        jnp.einsum("bgrst,btgd->bsgrd", d_scores, keys_rot, preferred_element_type=jnp.float32)
        * scale
    )
    d_keys_rot = (
        jnp.einsum("bgrst,bsgrd->btgd", d_scores, query_rot, preferred_element_type=jnp.float32)
        * scale
    )
    d_query = unrotate(d_query_rot.reshape(rows, H, HD), cosines, sines).reshape(rows, D)
    d_keys = unrotate(d_keys_rot.reshape(rows, KV, HD), cosines, sines).reshape(rows, kvw)
    d_qkv = jnp.concatenate(
        [d_query.astype(jnp.bfloat16), d_keys.astype(jnp.bfloat16), d_values], axis=1
    )
    grad_qkv = left_contract(normed, d_qkv)
    if whole_rows(w_query, D):
        sum_qkv = scatter_matrix(grad_qkv, False)
        sum_query = sum_qkv[:, :D]
        sum_key = sum_qkv[:, D : D + kvw]
        sum_value = sum_qkv[:, D + kvw :]
    else:
        sum_query = scatter_matrix(grad_qkv[:, :D], False)
        sum_key = scatter_matrix(grad_qkv[:, D : D + kvw], False)
        sum_value = scatter_matrix(grad_qkv[:, D + kvw :], False)
    d_normed = right_contract(d_qkv, mat_qkv)
    gain_one = jnp.sum(d_normed * inputs * factor_one, axis=0)
    d_inputs = (d_resid + norm_back(d_normed, inputs, factor_one, gain_attn)).astype(jnp.bfloat16)
    gains = total_over(jnp.stack([gain_one, gain_two]), scatter_order(True))
    return (
        result,
        d_inputs,
        sum_query.reshape(-1),
        sum_key.reshape(-1),
        sum_value.reshape(-1),
        sum_wout.reshape(-1),
        sum_gate.reshape(-1),
        sum_up.reshape(-1),
        sum_down.reshape(-1),
        gains[0],
        gains[1],
    )


def solution(mesh):
    placed = (
        P("dp", None),
        P("dp"),
        P("dp", None),
        P("dp"),
        P("dp"),
        P("dp"),
        P("dp"),
        P("dp"),
        P("dp"),
        P("dp"),
        P(),
        P(),
    )
    return jax.shard_map(
        body,
        mesh=mesh,
        in_specs=placed,
        out_specs=(
            P("dp", None),
            P("dp", None),
            P("dp"),
            P("dp"),
            P("dp"),
            P("dp"),
            P("dp"),
            P("dp"),
            P("dp"),
            P(),
            P(),
        ),
        check_vma=False,
    )
```

time: 1580 us -> 765 us (0.48)
  waiting for transfers between devices: 644 us -> 187 us
  blocking collectives: 222 us -> 0 us
  other arithmetic: 236 us -> 124 us
  local copies, waits for them, and re-layouts: 243 us -> 193 us
  starting transfers between devices: 0.46 us -> 45.3 us
    unnamed x2 -> x0, waiting for transfers between devices: 524 us -> none
    ppermute x0 -> x50, waiting for transfers between devices: none -> 187 us  [swap(): return lax.ppermute(value, 'dp', [(i, i ^ 1 << bit) for i in range(owners)])]
    all_gather x8 -> x0, other arithmetic: 184 us -> none  [the longest x2 82.5 us: micro_step(): lax.all_gather(shard_query, 'dp', axis=0, tiled=True)]
    all_gather x4 -> x0, blocking collectives: 180 us -> none  [the longest x2 92.1 us: micro_step(): lax.all_gather(shard_key, 'dp', axis=0, tiled=True)]
    all_gather x10 -> x0, waiting for transfers between devices: 116 us -> none  [the longest x2 86.4 us: micro_step(): lax.all_gather(shard_up, 'dp', axis=0, tiled=True)]
    reshape x24 -> x18, local copies, waits for them, and re-layouts: 131 us -> 41.9 us  [the longest x9 18.9 us: gather_rows(): jnp.concatenate([low, high], axis=1).reshape((shape[0] * 2,) + shape[1:])]
    while x363 -> x0, local copies, waits for them, and re-layouts: 53.9 us -> none
    another operation x4 -> x16, local copies, waits for them, and re-layouts: 0.37 us -> 52.3 us  [the longest x9 26.4 us: scatter_rows(): view = current.reshape(split)]
  transfers between devices with their start and end apart: 11 -> 50, of which waited for: 5 -> 23; matrix products, arithmetic and copies ran while one was open for 23% -> 38% of each run, Pallas kernels for 0% -> 0%
where the time goes in v1:
time: 765 us; the launch traced here: 759 us
  matrix products  208 us (27%)
  local copies, waits for them, and re-layouts  193 us (25%)
  waiting for transfers between devices  187 us (24%)
  other arithmetic  124 us (16%)
  starting transfers between devices  45.3 us (6%)
    ppermute x50, waiting for transfers between devices, swap(): return lax.ppermute(value, 'dp', [(i, i ^ 1 << bit) for i in range(owners)])  187 us
    dot_general x5, matrix products, right_contract(): lax.dot_general(first, second, (((1,), (1,)), ((), ())), preferred_elemen...  47.2 us
    ppermute x50, starting transfers between devices, swap(): return lax.ppermute(value, 'dp', [(i, i ^ 1 << bit) for i in range(owners)])  45.3 us
    dot_general x5, matrix products, matmul(): return jnp.dot(first, second, preferred_element_type=jnp.float32)  41 us
    dot_general x5, matrix products, left_contract(): lax.dot_general(first, second, (((0,), (0,)), ((), ())), preferred_elemen...  34.5 us
    concatenate x9, local copies, waits for them, and re-layouts, gather_rows(): jnp.concatenate([low, high], axis=1).reshape((shape[0] * 2,) + shape[1:])  30.7 us
    convert_element_type x20, other arithmetic, scatter_rows(): total = total.astype(jnp.bfloat16)  27.9 us
    another operation x9, local copies, waits for them, and re-layouts, scatter_rows(): view = current.reshape(split)  26.4 us
  transfers between devices with their start and end apart: 50, of which 23 were waited for; matrix products, arithmetic and copies ran while one was open for 38% of the time, Pallas kernels for 0%

profile of v1, /device:TPU:0, one launch (start us, length us, event | category | flops | bytes accessed | tf_op | source)
XLA Modules:
  0.0 759.1 jit_solution(8751859824216103092)
XLA Ops:
  28.9 45.7 %collective-permute-done.1 = bf16[2,30,2560]{2,1,0:T(8,128)(2,1)S(1)} collective-permute-done((bf16[2,30,2560]{2,1,0:T(8,128)(2,1)S(1)}, bf16[2,30,2560]{2,1,0:T(8,128)(2,1)S(1)}, u32[]{:S(2)}, u32[]{:S(2)}) %collective-permute-start.1) | collective-permute-done | bytes 307232 | tf_op jit(solution)/shard_map/ppermute | solution.py:82
  82.9 9.8 %collective-permute-done.2 = bf16[4,30,2560]{2,0,1:T(4,128)(2,1)S(1)} collective-permute-done((bf16[4,30,2560]{2,0,1:T(4,128)(2,1)S(1)}, bf16[4,30,2560]{2,0,1:T(4,128)(2,1)S(1)}, u32[]{:S(2)}, u32[]{:S(2)}) %collective-permute-start.2) | collective-permute-done | bytes 614432 | tf_op jit(solution)/shard_map/ppermute | solution.py:82
  120.3 16.1 %collective-permute-done.3 = bf16[8,30,2560]{2,0,1:T(8,128)(2,1)} collective-permute-done((bf16[8,30,2560]{2,0,1:T(8,128)(2,1)}, bf16[8,30,2560]{2,0,1:T(8,128)(2,1)}, u32[]{:S(2)}, u32[]{:S(2)}) %collective-permute-start.3) | collective-permute-done | bytes 1228832 | tf_op jit(solution)/shard_map/ppermute | solution.py:82
  147.7 11.4 %collective-permute-done.13 = bf16[8,30,2560]{2,0,1:T(8,128)(2,1)} collective-permute-done((bf16[8,30,2560]{2,0,1:T(8,128)(2,1)}, bf16[8,30,2560]{2,0,1:T(8,128)(2,1)}, u32[]{:S(2)}, u32[]{:S(2)}) %collective-permute-start.13) | collective-permute-done | bytes 1228832 | tf_op jit(solution)/shard_map/ppermute | solution.py:82
  189.3 7.5 reshape_reshape.94
  228.9 17.9 %fusion.98 = (f32[2,5,3,512]{3,2,1,0:T(4,128)S(1)}, f32[2,5,3,512,512]{3,4,2,1,0:T(8,128)}) fusion(pred[2,512,512]{1,2,0:T(8,128)(4,1)} %and_or_fusion, bf16[2,512,5,3,64]{1,4,3,2,0:T(8,128)(2,1)} %copy_dynamic-update-slice_fusion, bf16[2,512,5,32]{1,3,2,0:T(8,128)(2,1)} %get-tuple-element.99, bf16[2,512,5,32]{1,3,2,0:T(8,128)(2,1)} %get-tuple-element.100), kind=kOutput, calls=%fused_computation.276 | convolution fusion | flops 1039401472 | bytes 34664448 | tf_op jit(solution)/shard_map/sub | solution.py:242
  246.8 12.1 %convert_bitcast_fusion = bf16[2,512,5,3,64]{1,4,3,2,0:T(8,128)(2,1)S(1)} fusion(bf16[2,512,5,64,1]{1,0,3,2,4:T(2,128)(2,1)S(1)} %bitcast.495, f32[2,5,3,512,512]{3,4,2,1,0:T(8,128)} %get-tuple-element.90, f32[2,5,3,512]{3,2,1,0:T(4,128)S(1)} %get-tuple-element.89), kind=kOutput, calls=%fused_computation.96 | convolution fusion | flops 1023344640 | bytes 34140160 | tf_op jit(solution)/shard_map/bgrst,btgd->bsgrd/dot_general | solution.py:245
  284.0 7.7 %reshape_reshape.95 = bf16[960,2560]{1,0:T(8,128)(2,1)} reshape(bf16[16,2,1,30,2560]{4,3,1,0,2:T(8,128)(2,1)} %copy.388) | data formatting | bytes 9830400 | tf_op jit(solution)/shard_map/reshape;reshape | solution.py:158
  291.7 7.5 copy.401
  299.2 7.5 reshape_reshape.97
  306.7 11.1 %fusion.100 = f32[1024,2560]{1,0:T(8,128)} fusion(bf16[1024,960]{0,1:T(8,128)(2,1)} %multiply_convert_fusion.3, bf16[960,2560]{1,0:T(8,128)(2,1)} %reshape_reshape.97), kind=kOutput, calls=%fused_computation.278 | convolution fusion | flops 5033164800 | bytes 17367040 | tf_op jit(solution)/shard_map/dot_general | solution.py:58
  317.8 10.6 %fusion.99 = f32[1024,2560]{1,0:T(8,128)} fusion(bf16[1024,960]{0,1:T(8,128)(2,1)S(1)} %copy-done.25, bf16[960,2560]{1,0:T(8,128)(2,1)} %reshape_reshape.95), kind=kOutput, calls=%fused_computation.277 | convolution fusion | flops 5033164800 | bytes 17367040 | tf_op jit(solution)/shard_map/dot_general | solution.py:58
  333.3 18.7 %multiply_convert_fusion.1 = (bf16[1024,2560]{1,0:T(8,128)(2,1)}, bf16[1024,2560]{1,0:T(8,128)(2,1)}, bf16[1024,2560]{1,0:T(8,128)(2,1)}) fusion(f32[1024,2560]{1,0:T(8,128)} %fusion.99, f32[1024,2560]{1,0:T(8,128)} %fusion.100, bf16[2560,960]{1,0:T(8,128)(2,1)} %bitcast.464, bf16[1024,960]{0,1:T(8,128)(2,1)S(1)} %copy-done.22, f32[1024]{0:T(1024)S(1)} %copy-done.39), kind=kOutput, calls=%fused_computation.14 | convolution fusion | flops 5078056960 | bytes 43585536 | tf_op jit(solution)/shard_map/dot_general | solution.py:68
  352.0 10.4 %fusion.101 = f32[1024,960]{0,1:T(8,128)} fusion(bf16[1024,2560]{1,0:T(8,128)(2,1)} %get-tuple-element.19, bf16[960,2560]{1,0:T(8,128)(2,1)} %reshape_reshape.97), kind=kOutput, calls=%fused_computation.279 | convolution fusion | flops 5033164800 | bytes 14090240 | tf_op jit(solution)/shard_map/dot_general | solution.py:68
  362.4 7.0 convolution_convert_fusion.1
  369.4 8.3 %add_convert_fusion = bf16[1024,960]{0,1:T(8,128)(2,1)} fusion(f32[1024,960]{0,1:T(8,128)S(1)} %copy-done.4, bf16[1024,2560]{1,0:T(8,128)(2,1)} %get-tuple-element.18, bf16[2560,960]{1,0:T(8,128)(2,1)S(1)} %bitcast.467), kind=kOutput, calls=%fused_computation.57 | convolution fusion | flops 5035130880 | bytes 16056320 | tf_op jit(solution)/shard_map/dot_general | solution.py:58
  377.7 9.5 %convolution_convert_fusion = bf16[2560,960]{0,1:T(8,128)(2,1)} fusion(bf16[1024,2560]{1,0:T(8,128)(2,1)} %get-tuple-element.18, bf16[1024,960]{0,1:T(8,128)(2,1)S(1)} %copy-done.22, f32[1024]{0:T(1024)S(1)} %copy-done.39), kind=kOutput, calls=%fused_computation.26 | convolution fusion | flops 5038571520 | bytes 12128256 | tf_op jit(solution)/shard_map/dot_general | solution.py:62
  387.2 7.3 convolution_convert_fusion.2
  394.6 8.6 %multiply_reduce_fusion = (f32[960]{0:T(1024)}, f32[1024]{0:T(1024)S(1)}, f32[1024,960]{0,1:T(8,128)S(1)}) fusion(f32[1024,960]{0,1:T(8,128)S(1)} %copy-done.4, f32[1024]{0:T(1024)S(1)} %add_rsqrt_fusion, f32[960]{0:T(1024)S(1)} %copy-done.41, f32[1024,960]{0,1:T(8,128)} %fusion.101, bf16[1024,2560]{1,0:T(8,128)(2,1)S(1)} %bitcast.519, ...), kind=kOutput, calls=%fused_computation.51 | convolution fusion | flops 5040044032 | bytes 21970432 | tf_op jit(solution)/shard_map/dot_general | solution.py:68
  417.5 12.6 %fusion.63 = bf16[2,512,5,64]{1,3,2,0:T(8,128)(2,1)S(1)} fusion(bf16[2,512,5,3,64]{1,0,4,3,2:T(2,128)(2,1)S(1)} %reshape.1080, f32[2,5,3,512,512]{3,4,2,1,0:T(8,128)} %get-tuple-element.90, f32[2,5,3,512]{3,2,1,0:T(4,128)S(1)} %copy-done.35), kind=kOutput, calls=%fused_computation.124 | convolution fusion | flops 1022689280 | bytes 34140160 | tf_op jit(solution)/shard_map/bgrst,bsgrd->btgd/dot_general | solution.py:273
  430.2 23.5 %fusion.1 = (f32[2,5,3,512]{3,2,1,0:T(4,128)S(1)}, f32[2,5,512,512,3]{3,2,4,1,0:T(8,128)}) fusion(f32[2,5,3,512,512]{3,4,2,1,0:T(8,128)} %get-tuple-element.90, f32[2,5,3,512]{3,2,1,0:T(4,128)S(1)} %copy-done.35, bf16[2,512,5,3,64]{1,0,4,3,2:T(2,128)(2,1)S(1)} %reshape.1080, bf16[2,512,5,64,1]{1,0,3,2,4:T(2,128)(2,1)S(1)} %bitcast.496), kind=kOutput, calls=%fused_computation.3 | convolution fusion | flops 1030210560 | bytes 65658880 | tf_op jit(solution)/shard_map/bsgrd,btgd->bgrst/dot_general | solution.py:271
  453.6 26.4 %fusion.3 = bf16[2,5,3,512,512]{3,4,2,1,0:T(8,128)(2,1)} fusion(f32[2,5,512,512,3]{3,2,4,1,0:T(8,128)} %get-tuple-element.95, f32[2,5,3,512]{3,2,1,0:T(4,128)S(1)} %get-tuple-element.94, f32[2,5,3,512,512]{3,4,2,1,0:T(8,128)} %get-tuple-element.90, f32[2,5,3,512]{3,2,1,0:T(4,128)S(1)} %copy-done.35), kind=kLoop, calls=%fused_computation.5 | loop fusion | flops 31457280 | bytes 78766080 | tf_op jit(solution)/shard_map/convert_element_type | solution.py:276
  480.0 10.9 %fusion.56 = f32[2,5,8,8,512]{4,3,2,1,0:T(8,128)S(1)} fusion(bf16[2,512,5,3,64]{1,4,3,2,0:T(8,128)(2,1)} %copy_dynamic-update-slice_fusion, bf16[2,5,3,512,512]{3,4,2,1,0:T(8,128)(2,1)} %fusion.3), kind=kOutput, calls=%fused_computation.114 | convolution fusion | flops 1006960640 | bytes 19005440 | tf_op jit(solution)/shard_map/bgrst,bsgrd->btgd/dot_general | solution.py:282
  491.0 8.2 %multiply_bitcast_fusion = f32[2,512,5,3,64]{1,4,3,2,0:T(8,128)S(1)} fusion(bf16[2,5,3,512,512]{3,4,2,1,0:T(8,128)(2,1)} %fusion.3, bf16[2,512,5,32]{1,3,2,0:T(8,128)(2,1)S(1)} %copy-done.28, bf16[2,512,5,32]{1,3,2,0:T(8,128)(2,1)S(1)} %copy-done.29), kind=kOutput, calls=%fused_computation.52 | convolution fusion | flops 1008926720 | bytes 20316160 | tf_op jit(solution)/shard_map/bgrst,btgd->bsgrd/dot_general | solution.py:278
  505.0 6.7 reshape.1081
  522.6 7.2 convolution_convert_fusion.3
  532.6 7.8 %reshape_reshape.109 = bf16[16,2,1,30,2560]{4,3,1,0,2:T(8,128)(2,1)} reshape(bf16[960,2560]{1,0:T(8,128)(2,1)} %convolution_convert_fusion.1) | data formatting | bytes 9830400 | tf_op jit(solution)/shard_map/reshape;reshape | solution.py:113
  540.4 7.5 reshape_reshape.106
  547.9 7.9 %copy.434 = bf16[2560,960]{1,0:T(8,128)(2,1)} copy(bf16[2560,960]{0,1:T(8,128)(2,1)} %convolution_convert_fusion) | data formatting | bytes 9830400 | tf_op jit(solution)/shard_map/convert_element_type | solution.py:163
  590.9 6.9 collective-permute-done.26
  680.2 16.7 %collective-permute-done.41 = bf16[8,1,80,960]{3,2,0,1:T(8,128)(2,1)} collective-permute-done((bf16[8,1,80,960]{3,2,0,1:T(8,128)(2,1)}, bf16[8,1,80,960]{3,2,0,1:T(8,128)(2,1)}, u32[]{:S(2)}, u32[]{:S(2)}) %collective-permute-start.41) | collective-permute-done | bytes 1228832 | tf_op jit(solution)/shard_map/ppermute | solution.py:82
  717.1 17.7 %collective-permute-done.33 = bf16[1,2,30,2560]{3,2,1,0:T(8,128)(2,1)} collective-permute-done((bf16[1,2,30,2560]{3,2,1,0:T(8,128)(2,1)}, bf16[1,2,30,2560]{3,2,1,0:T(8,128)(2,1)}, u32[]{:S(2)}, u32[]{:S(2)}) %collective-permute-start.33) | collective-permute-done | bytes 307232 | tf_op jit(solution)/shard_map/ppermute | solution.py:82
  (433 shorter events, 362.2 us)
Async XLA Ops:
  2.7 17.8 %collective-permute-start.5 = (bf16[1,30,2560]{2,1,0:T(8,128)(2,1)}, bf16[1,30,2560]{2,1,0:T(8,128)(2,1)}, u32[]{:S(2)}, u32[]{:S(2)}) collective-permute-start(bf16[1,30,2560]{2,1,0:T(8,128)(2,1)} %convert_element_type.619), channel_id=1, source_target_pairs={{0,8},{1,9},{2,10},{3,11},{4,12},{5,13},{6,14},{7,15},{8,0},{9,1},... | collective-permute-start | bytes 460808 | tf_op jit(solution)/shard_map/ppermute | solution.py:82
  9.4 18.5 %collective-permute-start.15 = (bf16[1,80,960]{2,1,0:T(8,128)(2,1)}, bf16[1,80,960]{2,1,0:T(8,128)(2,1)}, u32[]{:S(2)}, u32[]{:S(2)}) collective-permute-start(bf16[1,80,960]{2,1,0:T(8,128)(2,1)} %convert_element_type.626), channel_id=1, source_target_pairs={{0,8},{1,9},{2,10},{3,11},{4,12},{5,13},{6,14},{7,15},{8,0},{9,1},... | collective-permute-start | bytes 460808 | tf_op jit(solution)/shard_map/ppermute | solution.py:82
  21.6 55.9 %collective-permute-start.6 = (bf16[2,30,2560]{2,1,0:T(8,128)(2,1)S(1)}, bf16[2,30,2560]{2,1,0:T(8,128)(2,1)S(1)}, u32[]{:S(2)}, u32[]{:S(2)}) collective-permute-start(bf16[2,30,2560]{2,1,0:T(8,128)(2,1)S(1)} %maximum_bitcast_fusion.2), channel_id=1, source_target_pairs={{0,16},{1,17},{2,18},{3,19},{4,20},{5,21},{6,22},{7,23},{8,24},{9,... | collective-permute-start | bytes 921608 | tf_op jit(solution)/shard_map/ppermute | solution.py:82
  24.7 50.5 %collective-permute-start.11 = (bf16[2,30,2560]{2,1,0:T(8,128)(2,1)S(1)}, bf16[2,30,2560]{2,1,0:T(8,128)(2,1)S(1)}, u32[]{:S(2)}, u32[]{:S(2)}) collective-permute-start(bf16[2,30,2560]{2,1,0:T(8,128)(2,1)S(1)} %maximum_bitcast_fusion.3), channel_id=1, source_target_pairs={{0,16},{1,17},{2,18},{3,19},{4,20},{5,21},{6,22},{7,23},{8,24},{9,... | collective-permute-start | bytes 921608 | tf_op jit(solution)/shard_map/ppermute | solution.py:82
  24.9 49.7 %collective-permute-start.1 = (bf16[2,30,2560]{2,1,0:T(8,128)(2,1)S(1)}, bf16[2,30,2560]{2,1,0:T(8,128)(2,1)S(1)}, u32[]{:S(2)}, u32[]{:S(2)}) collective-permute-start(bf16[2,30,2560]{2,1,0:T(8,128)(2,1)S(1)} %maximum_bitcast_fusion.1), channel_id=1, source_target_pairs={{0,16},{1,17},{2,18},{3,19},{4,20},{5,21},{6,22},{7,23},{8,24},{9,... | collective-permute-start | bytes 921608 | tf_op jit(solution)/shard_map/ppermute | solution.py:82
  28.8 52.1 %collective-permute-start.16 = (bf16[2,80,960]{2,1,0:T(8,128)(2,1)S(1)}, bf16[2,80,960]{2,1,0:T(8,128)(2,1)S(1)}, u32[]{:S(2)}, u32[]{:S(2)}) collective-permute-start(bf16[2,80,960]{2,1,0:T(8,128)(2,1)S(1)} %maximum_bitcast_fusion.4), channel_id=1, source_target_pairs={{0,16},{1,17},{2,18},{3,19},{4,20},{5,21},{6,22},{7,23},{8,24},{9,... | collective-permute-start | bytes 921608 | tf_op jit(solution)/shard_map/ppermute | solution.py:82
  75.9 16.9 %collective-permute-start.2 = (bf16[4,30,2560]{2,0,1:T(4,128)(2,1)S(1)}, bf16[4,30,2560]{2,0,1:T(4,128)(2,1)S(1)}, u32[]{:S(2)}, u32[]{:S(2)}) collective-permute-start(bf16[4,30,2560]{2,0,1:T(4,128)(2,1)S(1)} %copy.364), channel_id=1, source_target_pairs={{0,2},{1,3},{2,0},{3,1},{4,6},{5,7},{6,4},{7,5},{8,10},{9,11},{10,... | collective-permute-start | bytes 1843208 | tf_op jit(solution)/shard_map/ppermute | solution.py:82
  78.9 22.8 %collective-permute-start.7 = (bf16[4,30,2560]{2,0,1:T(4,128)(2,1)}, bf16[4,30,2560]{2,0,1:T(4,128)(2,1)}, u32[]{:S(2)}, u32[]{:S(2)}) collective-permute-start(bf16[4,30,2560]{2,0,1:T(4,128)(2,1)} %copy.383), channel_id=1, source_target_pairs={{0,4},{1,5},{2,6},{3,7},{4,0},{5,1},{6,2},{7,3},{8,12},{9,13},{10,... | collective-permute-start | bytes 1843208 | tf_op jit(solution)/shard_map/ppermute | solution.py:82
  80.4 22.6 %collective-permute-start.12 = (bf16[4,30,2560]{2,0,1:T(4,128)(2,1)S(1)}, bf16[4,30,2560]{2,0,1:T(4,128)(2,1)}, u32[]{:S(2)}, u32[]{:S(2)}) collective-permute-start(bf16[4,30,2560]{2,0,1:T(4,128)(2,1)S(1)} %copy.393), channel_id=1, source_target_pairs={{0,2},{1,3},{2,0},{3,1},{4,6},{5,7},{6,4},{7,5},{8,10},{9,11},{10,... | collective-permute-start | bytes 1843208 | tf_op jit(solution)/shard_map/ppermute | solution.py:82
  81.9 35.3 %collective-permute-start.17 = (bf16[4,80,960]{2,1,0:T(8,128)(2,1)}, bf16[4,80,960]{2,1,0:T(8,128)(2,1)}, u32[]{:S(2)}, u32[]{:S(2)}) collective-permute-start(bf16[4,80,960]{2,1,0:T(8,128)(2,1)} %bitcast.60), channel_id=1, source_target_pairs={{0,4},{1,5},{2,6},{3,7},{4,0},{5,1},{6,2},{7,3},{8,12},{9,13},{10,... | collective-permute-start | bytes 1843208 | tf_op jit(solution)/shard_map/ppermute | solution.py:82
  100.2 36.2 %collective-permute-start.3 = (bf16[8,30,2560]{2,0,1:T(8,128)(2,1)}, bf16[8,30,2560]{2,0,1:T(8,128)(2,1)}, u32[]{:S(2)}, u32[]{:S(2)}) collective-permute-start(bf16[8,30,2560]{2,0,1:T(8,128)(2,1)} %reshape.1057), channel_id=1, source_target_pairs={{0,4},{1,5},{2,6},{3,7},{4,0},{5,1},{6,2},{7,3},{8,12},{9,13},{10,... | collective-permute-start | bytes 3686408 | tf_op jit(solution)/shard_map/ppermute | solution.py:82
  114.5 44.6 %collective-permute-start.13 = (bf16[8,30,2560]{2,0,1:T(8,128)(2,1)}, bf16[8,30,2560]{2,0,1:T(8,128)(2,1)}, u32[]{:S(2)}, u32[]{:S(2)}) collective-permute-start(bf16[8,30,2560]{2,0,1:T(8,128)(2,1)} %reshape.1072), channel_id=1, source_target_pairs={{0,4},{1,5},{2,6},{3,7},{4,0},{5,1},{6,2},{7,3},{8,12},{9,13},{10,... | collective-permute-start | bytes 3686408 | tf_op jit(solution)/shard_map/ppermute | solution.py:82
  115.7 55.2 %collective-permute-start.8 = (bf16[8,30,2560]{2,0,1:T(8,128)(2,1)}, bf16[8,30,2560]{2,0,1:T(8,128)(2,1)}, u32[]{:S(2)}, u32[]{:S(2)}) collective-permute-start(bf16[8,30,2560]{2,0,1:T(8,128)(2,1)} %reshape.1067), channel_id=1, source_target_pairs={{0,2},{1,3},{2,0},{3,1},{4,6},{5,7},{6,4},{7,5},{8,10},{9,11},{10,... | collective-permute-start | bytes 3686408 | tf_op jit(solution)/shard_map/ppermute | solution.py:82
  119.8 58.9 %collective-permute-start.18 = (bf16[8,80,960]{2,1,0:T(8,128)(2,1)}, bf16[8,80,960]{2,1,0:T(8,128)(2,1)}, u32[]{:S(2)}, u32[]{:S(2)}) collective-permute-start(bf16[8,80,960]{2,1,0:T(8,128)(2,1)} %bitcast.64), channel_id=1, source_target_pairs={{0,2},{1,3},{2,0},{3,1},{4,6},{5,7},{6,4},{7,5},{8,10},{9,11},{10,... | collective-permute-start | bytes 3686408 | tf_op jit(solution)/shard_map/ppermute | solution.py:82
  147.7 33.3 %collective-permute-start.4 = (bf16[16,30,2560]{2,0,1:T(8,128)(2,1)}, bf16[16,30,2560]{2,0,1:T(8,128)(2,1)}, u32[]{:S(2)}, u32[]{:S(2)}) collective-permute-start(bf16[16,30,2560]{2,0,1:T(8,128)(2,1)} %reshape.1059), channel_id=1, source_target_pairs={{0,1},{1,0},{2,3},{3,2},{4,5},{5,4},{6,7},{7,6},{8,9},{9,8},{10,11... | collective-permute-start | bytes 7372808 | tf_op jit(solution)/shard_map/ppermute | solution.py:82
  178.1 89.1 %collective-permute-start.9 = (bf16[16,30,2560]{2,0,1:T(8,128)(2,1)}, bf16[16,30,2560]{2,0,1:T(8,128)(2,1)}, u32[]{:S(2)}, u32[]{:S(2)}) collective-permute-start(bf16[16,30,2560]{2,0,1:T(8,128)(2,1)} %reshape.1068), channel_id=1, source_target_pairs={{0,1},{1,0},{2,3},{3,2},{4,5},{5,4},{6,7},{7,6},{8,9},{9,8},{10,11... | collective-permute-start | bytes 7372808 | tf_op jit(solution)/shard_map/ppermute | solution.py:82
  178.2 93.7 %collective-permute-start.14 = (bf16[16,30,2560]{2,0,1:T(8,128)(2,1)}, bf16[16,30,2560]{2,0,1:T(8,128)(2,1)}, u32[]{:S(2)}, u32[]{:S(2)}) collective-permute-start(bf16[16,30,2560]{2,0,1:T(8,128)(2,1)} %reshape.1074), channel_id=1, source_target_pairs={{0,1},{1,0},{2,3},{3,2},{4,5},{5,4},{6,7},{7,6},{8,9},{9,8},{10,11... | collective-permute-start | bytes 7372808 | tf_op jit(solution)/shard_map/ppermute | solution.py:82
  180.8 147.5 %collective-permute-start.19 = (bf16[16,80,960]{2,1,0:T(8,128)(2,1)S(1)}, bf16[16,80,960]{2,1,0:T(8,128)(2,1)}, u32[]{:S(2)}, u32[]{:S(2)}) collective-permute-start(bf16[16,80,960]{2,1,0:T(8,128)(2,1)S(1)} %bitcast.456), channel_id=1, source_target_pairs={{0,1},{1,0},{2,3},{3,2},{4,5},{5,4},{6,7},{7,6},{8,9},{9,8},{10,11... | collective-permute-start | bytes 7372808 | tf_op jit(solution)/shard_map/ppermute | solution.py:82
  557.4 26.3 %collective-permute-start.25 = (bf16[16,1,30,960]{3,0,2,1:T(8,128)(2,1)}, bf16[16,1,30,960]{3,0,2,1:T(8,128)(2,1)}, u32[]{:S(2)}, u32[]{:S(2)}) collective-permute-start(bf16[16,1,30,960]{3,0,2,1:T(8,128)(2,1)} %bitcast.436), channel_id=1, source_target_pairs={{0,1},{1,0},{2,3},{3,2},{4,5},{5,4},{6,7},{7,6},{8,9},{9,8},{10,11... | collective-permute-start | bytes 2764808 | tf_op jit(solution)/shard_map/ppermute | solution.py:82
  565.0 60.9 %collective-permute-start.30 = (bf16[16,1,30,2560]{3,0,2,1:T(8,128)(2,1)}, bf16[16,1,30,2560]{3,0,2,1:T(8,128)(2,1)}, u32[]{:S(2)}, u32[]{:S(2)}) collective-permute-start(bf16[16,1,30,2560]{3,0,2,1:T(8,128)(2,1)} %bitcast.432), channel_id=1, source_target_pairs={{0,1},{1,0},{2,3},{3,2},{4,5},{5,4},{6,7},{7,6},{8,9},{9,8},{10,11... | collective-permute-start | bytes 7372808 | tf_op jit(solution)/shard_map/ppermute | solution.py:82
  569.9 64.0 %collective-permute-start.35 = (bf16[16,1,30,2560]{3,0,2,1:T(8,128)(2,1)}, bf16[16,1,30,2560]{3,0,2,1:T(8,128)(2,1)}, u32[]{:S(2)}, u32[]{:S(2)}) collective-permute-start(bf16[16,1,30,2560]{3,0,2,1:T(8,128)(2,1)} %bitcast.431), channel_id=1, source_target_pairs={{0,1},{1,0},{2,3},{3,2},{4,5},{5,4},{6,7},{7,6},{8,9},{9,8},{10,11... | collective-permute-start | bytes 7372808 | tf_op jit(solution)/shard_map/ppermute | solution.py:82
  574.5 24.1 %collective-permute-start.20 = (bf16[16,1,30,1600]{3,0,2,1:T(8,128)(2,1)S(1)}, bf16[16,1,30,1600]{3,0,2,1:T(8,128)(2,1)S(1)}, u32[]{:S(2)}, u32[]{:S(2)}) collective-permute-start(bf16[16,1,30,1600]{3,0,2,1:T(8,128)(2,1)S(1)} %bitcast.487), channel_id=1, source_target_pairs={{0,1},{1,0},{2,3},{3,2},{4,5},{5,4},{6,7},{7,6},{8,9},{9,8},{10,11... | collective-permute-start | bytes 4608008 | tf_op jit(solution)/shard_map/ppermute | solution.py:82
  590.8 51.0 %collective-permute-start.40 = (bf16[16,1,80,960]{3,2,0,1:T(8,128)(2,1)}, bf16[16,1,80,960]{3,2,0,1:T(8,128)(2,1)}, u32[]{:S(2)}, u32[]{:S(2)}) collective-permute-start(bf16[16,1,80,960]{3,2,0,1:T(8,128)(2,1)} %dynamic-slice_bitcast_fusion), channel_id=1, source_target_pairs={{0,1},{1,0},{2,3},{3,2},{4,5},{5,4},{6,7},{7,6},{8,9},{9,8},{10,11... | collective-permute-start | bytes 7372808 | tf_op jit(solution)/shard_map/ppermute | solution.py:82
  632.3 27.4 %collective-permute-start.31 = (bf16[4,2,30,2560]{3,0,2,1:T(4,128)(2,1)}, bf16[4,2,30,2560]{3,0,2,1:T(4,128)(2,1)}, u32[]{:S(2)}, u32[]{:S(2)}) collective-permute-start(bf16[4,2,30,2560]{3,0,2,1:T(4,128)(2,1)} %bitcast.435), channel_id=1, source_target_pairs={{0,4},{1,5},{2,6},{3,7},{4,0},{5,1},{6,2},{7,3},{8,12},{9,13},{10,... | collective-permute-start | bytes 3686408 | tf_op jit(solution)/shard_map/ppermute | solution.py:82
  639.4 30.3 %collective-permute-start.36 = (bf16[8,1,30,2560]{3,0,2,1:T(8,128)(2,1)}, bf16[8,1,30,2560]{3,0,2,1:T(8,128)(2,1)}, u32[]{:S(2)}, u32[]{:S(2)}) collective-permute-start(bf16[8,1,30,2560]{3,0,2,1:T(8,128)(2,1)} %bitcast.434), channel_id=1, source_target_pairs={{0,2},{1,3},{2,0},{3,1},{4,6},{5,7},{6,4},{7,5},{8,10},{9,11},{10,... | collective-permute-start | bytes 3686408 | tf_op jit(solution)/shard_map/ppermute | solution.py:82
  651.8 45.1 %collective-permute-start.41 = (bf16[8,1,80,960]{3,2,0,1:T(8,128)(2,1)}, bf16[8,1,80,960]{3,2,0,1:T(8,128)(2,1)}, u32[]{:S(2)}, u32[]{:S(2)}) collective-permute-start(bf16[8,1,80,960]{3,2,0,1:T(8,128)(2,1)} %dynamic-slice_bitcast_fusion.1), channel_id=1, source_target_pairs={{0,2},{1,3},{2,0},{3,1},{4,6},{5,7},{6,4},{7,5},{8,10},{9,11},{10,... | collective-permute-start | bytes 3686408 | tf_op jit(solution)/shard_map/ppermute | solution.py:82
  662.4 41.0 %collective-permute-start.32 = (bf16[4,1,30,2560]{3,0,2,1:T(4,128)(2,1)S(1)}, bf16[4,1,30,2560]{3,0,2,1:T(4,128)(2,1)}, u32[]{:S(2)}, u32[]{:S(2)}) collective-permute-start(bf16[4,1,30,2560]{3,0,2,1:T(4,128)(2,1)S(1)} %constant_dynamic-slice_fusion.12), channel_id=1, source_target_pairs={{0,2},{1,3},{2,0},{3,1},{4,6},{5,7},{6,4},{7,5},{8,10},{9,11},{10,... | collective-permute-start | bytes 1843208 | tf_op jit(solution)/shard_map/ppermute | solution.py:82
  679.7 30.7 %collective-permute-start.37 = (bf16[4,1,30,2560]{3,0,2,1:T(4,128)(2,1)}, bf16[4,1,30,2560]{3,0,2,1:T(4,128)(2,1)}, u32[]{:S(2)}, u32[]{:S(2)}) collective-permute-start(bf16[4,1,30,2560]{3,0,2,1:T(4,128)(2,1)} %bitcast.438), channel_id=1, source_target_pairs={{0,4},{1,5},{2,6},{3,7},{4,0},{5,1},{6,2},{7,3},{8,12},{9,13},{10,... | collective-permute-start | bytes 1843208 | tf_op jit(solution)/shard_map/ppermute | solution.py:82
  708.2 26.6 %collective-permute-start.33 = (bf16[1,2,30,2560]{3,2,1,0:T(8,128)(2,1)}, bf16[1,2,30,2560]{3,2,1,0:T(8,128)(2,1)}, u32[]{:S(2)}, u32[]{:S(2)}) collective-permute-start(bf16[1,2,30,2560]{3,2,1,0:T(8,128)(2,1)} %bitcast.441), channel_id=1, source_target_pairs={{0,16},{1,17},{2,18},{3,19},{4,20},{5,21},{6,22},{7,23},{8,24},{9,... | collective-permute-start | bytes 921608 | tf_op jit(solution)/shard_map/ppermute | solution.py:82
  712.7 29.1 %collective-permute-start.38 = (bf16[1,2,30,2560]{3,2,1,0:T(8,128)(2,1)S(1)}, bf16[1,2,30,2560]{3,2,1,0:T(8,128)(2,1)S(1)}, u32[]{:S(2)}, u32[]{:S(2)}) collective-permute-start(bf16[1,2,30,2560]{3,2,1,0:T(8,128)(2,1)S(1)} %bitcast.502), channel_id=1, source_target_pairs={{0,16},{1,17},{2,18},{3,19},{4,20},{5,21},{6,22},{7,23},{8,24},{9,... | collective-permute-start | bytes 921608 | tf_op jit(solution)/shard_map/ppermute | solution.py:82
  714.8 32.7 %collective-permute-start.43 = (bf16[1,2,80,960]{3,2,1,0:T(8,128)(2,1)S(1)}, bf16[1,2,80,960]{3,2,1,0:T(8,128)(2,1)S(1)}, u32[]{:S(2)}, u32[]{:S(2)}) collective-permute-start(bf16[1,2,80,960]{3,2,1,0:T(8,128)(2,1)S(1)} %dynamic-slice_bitcast_fusion.4), channel_id=1, source_target_pairs={{0,16},{1,17},{2,18},{3,19},{4,20},{5,21},{6,22},{7,23},{8,24},{9,... | collective-permute-start | bytes 921608 | tf_op jit(solution)/shard_map/ppermute | solution.py:82
  735.9 15.2 %collective-permute-start.34 = (bf16[1,1,30,2560]{3,2,1,0:T(8,128)(2,1)S(1)}, bf16[1,1,30,2560]{3,2,1,0:T(8,128)(2,1)S(1)}, u32[]{:S(2)}, u32[]{:S(2)}) collective-permute-start(bf16[1,1,30,2560]{3,2,1,0:T(8,128)(2,1)S(1)} %constant_dynamic-slice_fusion.9), channel_id=1, source_target_pairs={{0,8},{1,9},{2,10},{3,11},{4,12},{5,13},{6,14},{7,15},{8,0},{9,1},... | collective-permute-start | bytes 460808 | tf_op jit(solution)/shard_map/ppermute | solution.py:82
  (77 other events, 1255.5 us)

commit v2 on v1

--- a/solution.py
+++ b/solution.py
@@ -103,24 +103,41 @@
     return current
 
 
-def scatter_rows(parts, order):
-    current = parts
-    left = list(range(len(order)))
-    for step, bit in enumerate(order):
-        place = sum(1 for b in left if b > bit)
-        shape = current.shape
-        split = (1 << place, 2, shape[0] >> (place + 1)) + shape[1:]
-        view = current.reshape(split)
+class Halving:
+    def __init__(self, parts, order):
+        self.current = parts
+        self.order = list(order)
+        self.left = sorted(order)
+
+    def step(self):
+        if not self.order:
+            return
+        bit = self.order.pop(0)
+        place = sum(1 for b in self.left if b > bit)
+        shape = self.current.shape
+        view = self.current.reshape((1 << place, 2, shape[0] >> (place + 1)) + shape[1:])
         mine = my_bit(bit)
         sent = lax.dynamic_index_in_dim(view, 1 - mine, 1, keepdims=False)
         kept = lax.dynamic_index_in_dim(view, mine, 1, keepdims=False)
         got = swap(sent, bit)
         total = kept.astype(jnp.float32) + got.astype(jnp.float32)
-        if step < len(order) - 1:
+        if self.order:
             total = total.astype(jnp.bfloat16)
-        current = total.reshape((shape[0] // 2,) + shape[1:])
-        left.remove(bit)
-    return current[0]
+        self.current = total.reshape((shape[0] // 2,) + shape[1:])
+        self.left.remove(bit)
+
+    def finish(self):
+        while self.order:
+            self.step()
+        return self.current[0]
+
+
+def advance(chains, *values):
+    held, values = lax.optimization_barrier((tuple(c.current for c in chains), values))
+    for chain, current in zip(chains, held):
+        chain.current = current
+        chain.step()
+    return values if len(values) > 1 else values[0]
 
 
 def total_over(value, order):
@@ -145,6 +162,26 @@
 def scatter_order(flip):
     core, near, far = orders()
     return core + (near[::-1] if flip else near) + far[::-1]
+
+
+def padded(height):
+    return -(-height // 16) * 16
+
+
+def spread(height, owners):
+    pad = padded(height)
+    row = lax.broadcasted_iota(jnp.int32, (height * owners, owners * pad), 0)
+    column = lax.broadcasted_iota(jnp.int32, (height * owners, owners * pad), 1)
+    inner = column % pad
+    hit = (inner < height) & (row == column // pad * height + inner)
+    return hit.astype(jnp.bfloat16)
+
+
+def gather_padded(shard, chosen, flip):
+    height = shard.shape[0]
+    shard = jnp.pad(shard.astype(jnp.bfloat16), ((0, padded(height) - height), (0, 0)))
+    full = gather_rows(shard, gather_order(flip))
+    return matmul(chosen, full.reshape(-1, shard.shape[1])).astype(jnp.bfloat16)
 
 
 def whole_rows(flat, width):
@@ -165,7 +202,7 @@
         parts = grad.reshape(owners, grad.shape[0] // owners, grad.shape[1])
     else:
         parts = grad.reshape(owners, -1)
-    return scatter_rows(parts, scatter_order(flip))
+    return Halving(parts, scatter_order(flip))
 
 
 def attend(query_rot, keys_rot, values, allowed, scale):
@@ -196,7 +233,10 @@
     scale = 1.0 / math.sqrt(HD)
     rows = tokens.shape[0]
     blocks = rows // slots
-    if whole_rows(w_query, D):
+    height = w_query.shape[0] // D
+    aligned = whole_rows(w_query, D)
+    if aligned:
+        chosen = spread(height, lax.axis_size("dp"))
         joined = jnp.concatenate(
             [
                 w_query.reshape(-1, D),
@@ -205,8 +245,8 @@
                 w_out.reshape(-1, D),
             ],
             axis=1,
-        ).astype(jnp.bfloat16)
-        joined = gather_rows(joined, gather_order(False)).reshape(D, D + 2 * kvw + D)
+        )
+        joined = gather_padded(joined, chosen, False)
         mat_qkv = joined[:, : D + 2 * kvw]
         mat_out = joined[:, D + 2 * kvw :]
     else:
@@ -219,8 +259,16 @@
             axis=1,
         )
         mat_out = gather_matrix(w_out, D, False)
-    mat_gate = gather_matrix(w_gate, FF, True)
-    mat_up = gather_matrix(w_up, FF, False)
+    if aligned:
+        mat_gate = gather_padded(w_gate.reshape(-1, FF), chosen, True)
+        mat_up = gather_padded(w_up.reshape(-1, FF), chosen, False)
+    else:
+        mat_gate = gather_matrix(w_gate, FF, True)
+        mat_up = gather_matrix(w_up, FF, False)
+
+    def widen(value):
+        return matmul(value, chosen).astype(jnp.bfloat16) if aligned else value
+
     mat_down = gather_matrix(w_down, D, True)
 
     allowed, placed, living = jax.vmap(block_mask)(position.reshape(blocks, slots))
@@ -247,6 +295,7 @@
     resid = inputs + matmul(mixed, mat_out)
     factor_two = lax.rsqrt(jnp.mean(resid * resid, axis=-1, keepdims=True) + EPS)
     normed_two = (resid * factor_two * gain_mlp).astype(jnp.bfloat16)
+    wide_two = widen(normed_two)
     gate = matmul(normed_two, mat_gate)
     upper = matmul(normed_two, mat_up)
     sigma = jax.nn.sigmoid(gate)
@@ -255,25 +304,31 @@
 
     grad_out = cotangent.astype(jnp.float32) * living[:, None].astype(jnp.float32)
     grad_out_b = grad_out.astype(jnp.bfloat16)
-    sum_down = scatter_matrix(left_contract(hidden, grad_out_b), False)
+    down = scatter_matrix(left_contract(hidden, grad_out_b), False)
+    grad_out_b = advance([down], grad_out_b)
     d_hidden = right_contract(grad_out_b, mat_down)
     d_upper = (d_hidden * gate * sigma).astype(jnp.bfloat16)
     d_gate = (d_hidden * upper * sigma * (1.0 + gate * (1.0 - sigma))).astype(jnp.bfloat16)
-    sum_gate = scatter_matrix(left_contract(normed_two, d_gate), True)
-    sum_up = scatter_matrix(left_contract(normed_two, d_upper), False)
+    d_upper, d_gate = advance([down], d_upper, d_gate)
+    gated = scatter_matrix(left_contract(wide_two, d_gate), True)
+    raised = scatter_matrix(left_contract(wide_two, d_upper), False)
+    d_upper, d_gate = advance([gated, raised, down], d_upper, d_gate)
     d_normed_two = right_contract(d_gate, mat_gate) + right_contract(d_upper, mat_up)
     gain_two = jnp.sum(d_normed_two * resid * factor_two, axis=0)
     d_resid = grad_out + norm_back(d_normed_two, resid, factor_two, gain_mlp)
     d_attn = d_resid.astype(jnp.bfloat16)
-    sum_wout = scatter_matrix(left_contract(mixed, d_attn), True)
+    d_attn = advance([gated], d_attn)
+    wout = scatter_matrix(left_contract(widen(mixed), d_attn), True)
     d_mixed = right_contract(d_attn, mat_out).astype(jnp.bfloat16)
     d_mixed = d_mixed.reshape(blocks, slots, KV, groups, HD)
+    d_mixed = advance([wout, raised, down], d_mixed)
     d_probs = jnp.einsum("bsgrd,btgd->bgrst", d_mixed, values, preferred_element_type=jnp.float32)
     probs_back = expd / total_exp
     d_values = jnp.einsum("bgrst,bsgrd->btgd", probs, d_mixed, preferred_element_type=jnp.float32)
     d_values = d_values.reshape(rows, kvw).astype(jnp.bfloat16)
     d_scores = probs_back * (d_probs - jnp.sum(probs_back * d_probs, axis=-1, keepdims=True))
     d_scores = d_scores.astype(jnp.bfloat16)
+    d_scores = advance([wout, gated, raised, down], d_scores)
     d_query_rot = (
         jnp.einsum("bgrst,btgd->bsgrd", d_scores, keys_rot, preferred_element_type=jnp.float32)
         * scale
@@ -282,25 +337,33 @@
         jnp.einsum("bgrst,bsgrd->btgd", d_scores, query_rot, preferred_element_type=jnp.float32)
         * scale
     )
+    d_query_rot, d_keys_rot = advance([wout, gated, raised], d_query_rot, d_keys_rot)
     d_query = unrotate(d_query_rot.reshape(rows, H, HD), cosines, sines).reshape(rows, D)
     d_keys = unrotate(d_keys_rot.reshape(rows, KV, HD), cosines, sines).reshape(rows, kvw)
     d_qkv = jnp.concatenate(
         [d_query.astype(jnp.bfloat16), d_keys.astype(jnp.bfloat16), d_values], axis=1
     )
-    grad_qkv = left_contract(normed, d_qkv)
-    if whole_rows(w_query, D):
-        sum_qkv = scatter_matrix(grad_qkv, False)
-        sum_query = sum_qkv[:, :D]
-        sum_key = sum_qkv[:, D : D + kvw]
-        sum_value = sum_qkv[:, D + kvw :]
-    else:
-        sum_query = scatter_matrix(grad_qkv[:, :D], False)
-        sum_key = scatter_matrix(grad_qkv[:, D : D + kvw], False)
-        sum_value = scatter_matrix(grad_qkv[:, D + kvw :], False)
+    d_qkv = advance([wout, gated, raised], d_qkv)
+    grad_qkv = left_contract(widen(normed), d_qkv)
+    if aligned:
+        joint = scatter_matrix(grad_qkv, False)
+        d_qkv = advance([joint, wout], d_qkv)
     d_normed = right_contract(d_qkv, mat_qkv)
     gain_one = jnp.sum(d_normed * inputs * factor_one, axis=0)
     d_inputs = (d_resid + norm_back(d_normed, inputs, factor_one, gain_attn)).astype(jnp.bfloat16)
     gains = total_over(jnp.stack([gain_one, gain_two]), scatter_order(True))
+    if aligned:
+        sum_qkv = joint.finish()[:height]
+        sum_query = sum_qkv[:, :D]
+        sum_key = sum_qkv[:, D : D + kvw]
+        sum_value = sum_qkv[:, D + kvw :]
+        sum_wout, sum_gate, sum_up = [c.finish()[:height] for c in (wout, gated, raised)]
+    else:
+        sum_query = scatter_matrix(grad_qkv[:, :D], False).finish()
+        sum_key = scatter_matrix(grad_qkv[:, D : D + kvw], False).finish()
+        sum_value = scatter_matrix(grad_qkv[:, D + kvw :], False).finish()
+        sum_wout, sum_gate, sum_up = wout.finish(), gated.finish(), raised.finish()
+    sum_down = down.finish()
     return (
         result,
         d_inputs,

time: 765 us -> 667 us (0.87)
  local copies, waits for them, and re-layouts: 193 us -> 88.5 us
  other arithmetic: 124 us -> 79.7 us
  matrix products: 208 us -> 248 us
  starting transfers between devices: 45.3 us -> 54.1 us
    another operation x15 -> x0, local copies, waits for them, and re-layouts: 51.4 us -> none  [the longest x9 26.4 us: scatter_rows(): view = current.reshape(split)]
    convert_element_type x21 -> x10, other arithmetic: 54.2 us -> 11.5 us  [the longest x6 4.93 us: step(): total = total.astype(jnp.bfloat16)]
    sub x0 -> x1, matrix products: none -> 33.3 us  [body(): d_probs - jnp.sum(probs_back * d_probs, axis=-1, keepdims=True)]
    concatenate x9 -> x6, local copies, waits for them, and re-layouts: 30.7 us -> 2.05 us  [gather_rows(): jnp.concatenate([low, high], axis=1).reshape((shape[0] * 2,) + shape[1:])]
    reshape x0 -> x14, other arithmetic: none -> 24 us  [step(): self.current = total.reshape((shape[0] // 2,) + shape[1:])]
    dot_general x1 -> x0, matrix products: 23.5 us -> none  [body(): jnp.einsum('bsgrd,btgd->bgrst', d_mixed, values, preferred_element_type=j...]
    dot_general x5 -> x9, matrix products: 41 us -> 63.9 us  [matmul(): return jnp.dot(first, second, preferred_element_type=jnp.float32)]
    reshape x11 -> x7, local copies, waits for them, and re-layouts: 25.1 us -> 2.67 us  [the longest x1 0.75 us: body(): sum_wout.reshape(-1)]
  transfers between devices with their start and end apart: 50 -> 50, of which waited for: 23 -> 23; matrix products, arithmetic and copies ran while one was open for 38% -> 48% of each run, Pallas kernels for 0% -> 0%
where the time goes in v2:
time: 667 us; the launch traced here: 656 us
  matrix products  248 us (37%)
  waiting for transfers between devices  183 us (27%)
  local copies, waits for them, and re-layouts  88.5 us (13%)
  other arithmetic  79.7 us (12%)
  starting transfers between devices  54.1 us (8%)
    ppermute x50, waiting for transfers between devices, swap(): return lax.ppermute(value, 'dp', [(i, i ^ 1 << bit) for i in range(owners)])  183 us
    dot_general x9, matrix products, matmul(): return jnp.dot(first, second, preferred_element_type=jnp.float32)  63.9 us
    ppermute x50, starting transfers between devices, swap(): return lax.ppermute(value, 'dp', [(i, i ^ 1 << bit) for i in range(owners)])  54.1 us
    dot_general x5, matrix products, right_contract(): lax.dot_general(first, second, (((1,), (1,)), ((), ())), preferred_elemen...  50.2 us
    dot_general x5, matrix products, left_contract(): lax.dot_general(first, second, (((0,), (0,)), ((), ())), preferred_elemen...  37 us
    sub x1, matrix products, body(): d_probs - jnp.sum(probs_back * d_probs, axis=-1, keepdims=True)  33.3 us
    reshape x14, other arithmetic, step(): self.current = total.reshape((shape[0] // 2,) + shape[1:])  24 us
    squeeze x25, local copies, waits for them, and re-layouts, step(): sent = lax.dynamic_index_in_dim(view, 1 - mine, 1, keepdims=False)  18.4 us
  transfers between devices with their start and end apart: 50, of which 23 were waited for; matrix products, arithmetic and copies ran while one was open for 48% of the time, Pallas kernels for 0%

profile of v2, /device:TPU:0, one launch (start us, length us, event | category | flops | bytes accessed | tf_op | source)
XLA Modules:
  0.0 656.3 jit_solution(12336538287350442454)
XLA Ops:
  32.8 30.7 %collective-permute-done.16 = bf16[2,80,960]{2,1,0:T(8,128)(2,1)S(1)} collective-permute-done((bf16[2,80,960]{2,1,0:T(8,128)(2,1)S(1)}, bf16[2,80,960]{2,1,0:T(8,128)(2,1)S(1)}, u32[]{:S(2)}, u32[]{:S(2)}) %collective-permute-start.16) | collective-permute-done | bytes 307232 | tf_op jit(solution)/shard_map/ppermute | solution.py:82
  87.8 7.6 %collective-permute-done.7 = bf16[4,32,2560]{2,1,0:T(8,128)(2,1)S(1)} collective-permute-done((bf16[4,32,2560]{2,1,0:T(8,128)(2,1)S(1)}, bf16[4,32,2560]{2,1,0:T(8,128)(2,1)S(1)}, u32[]{:S(2)}, u32[]{:S(2)}) %collective-permute-start.7) | collective-permute-done | bytes 655392 | tf_op jit(solution)/shard_map/ppermute | solution.py:82
  103.2 26.2 %collective-permute-done.18 = bf16[8,80,960]{2,1,0:T(8,128)(2,1)S(1)} collective-permute-done((bf16[8,80,960]{2,1,0:T(8,128)(2,1)S(1)}, bf16[8,80,960]{2,1,0:T(8,128)(2,1)S(1)}, u32[]{:S(2)}, u32[]{:S(2)}) %collective-permute-start.18) | collective-permute-done | bytes 1228832 | tf_op jit(solution)/shard_map/ppermute | solution.py:82
  131.1 24.2 %collective-permute-done.8 = bf16[8,32,2560]{2,1,0:T(8,128)(2,1)S(1)} collective-permute-done((bf16[8,32,2560]{2,1,0:T(8,128)(2,1)S(1)}, bf16[8,32,2560]{2,1,0:T(8,128)(2,1)S(1)}, u32[]{:S(2)}, u32[]{:S(2)}) %collective-permute-start.8) | collective-permute-done | bytes 1310752 | tf_op jit(solution)/shard_map/ppermute | solution.py:82
  194.7 17.7 %fusion.151 = (f32[2,5,3,512]{3,2,1,0:T(4,128)S(1)}, f32[2,5,3,512,512]{3,4,2,1,0:T(8,128)}) fusion(pred[2,512,512]{1,2,0:T(8,128)(4,1)} %and_or_fusion, bf16[2,512,5,3,64]{1,4,3,2,0:T(8,128)(2,1)} %copy_dynamic-update-slice_fusion, bf16[2,512,5,32]{1,3,2,0:T(8,128)(2,1)S(1)} %bitcast.602, bf16[2,512,5,32]{1,3,2,0:T(8,128)(2,1)S(1)} %bitcast.604), kind=kOutput, calls=%fused_computation.301 | convolution fusion | flops 1039401472 | bytes 34664448 | tf_op jit(solution)/shard_map/sub | solution.py:290
  212.5 11.9 %convert_bitcast_fusion = bf16[2,512,5,3,64]{1,4,3,2,0:T(8,128)(2,1)S(1)} fusion(bf16[2,512,5,64,1]{1,0,3,2,4:T(2,128)(2,1)} %bitcast.608, f32[2,5,3,512,512]{3,4,2,1,0:T(8,128)} %get-tuple-element.149, f32[2,5,3,512]{3,2,1,0:T(4,128)S(1)} %get-tuple-element.148), kind=kOutput, calls=%fused_computation.111 | convolution fusion | flops 1023344640 | bytes 34140160 | tf_op jit(solution)/shard_map/bgrst,btgd->bsgrd/dot_general | solution.py:293
  236.8 6.9 %convolution_convert_fusion.3 = bf16[960,2560]{1,0:T(8,128)(2,1)} fusion(bf16[1024,2560]{1,0:T(8,128)(2,1)S(1)} %bitcast.560, s32[1024]{0:T(1024)S(1)} %get-tuple-element.160, s32[1024]{0:T(1024)S(1)} %get-tuple-element.163, s32[1024]{0:T(1024)S(1)} %get-tuple-element.161, s32[1024]{0:T(1024)S(1)} %get-tuple-element.162, ...), kind=kOutput, calls=%fused_computation.33 | convolution fusion | flops 5042503680 | bytes 10176512 | tf_op jit(solution)/shard_map/dot_general | solution.py:58
  246.8 7.1 %convolution_convert_fusion.2 = bf16[960,2560]{1,0:T(8,128)(2,1)} fusion(bf16[1024,2560]{1,0:T(8,128)(2,1)S(1)} %bitcast.562, s32[1024]{0:T(1024)S(1)} %get-tuple-element.160, s32[1024]{0:T(1024)S(1)} %get-tuple-element.163, s32[1024]{0:T(1024)S(1)} %get-tuple-element.161, s32[1024]{0:T(1024)S(1)} %get-tuple-element.162, ...), kind=kOutput, calls=%fused_computation.32 | convolution fusion | flops 5042503680 | bytes 10176512 | tf_op jit(solution)/shard_map/dot_general | solution.py:58
  254.3 5.7 fusion.152
  260.0 16.2 %multiply_convert_fusion.2 = (bf16[1024,2560]{1,0:T(8,128)(2,1)S(1)}, f32[1024,2560]{1,0:T(8,128)}) fusion(f32[1024,2560]{1,0:T(8,128)S(1)} %fusion.152, bf16[1024,960]{0,1:T(8,128)(2,1)S(1)} %multiply_convert_fusion.3, bf16[960,2560]{1,0:T(8,128)(2,1)} %convolution_convert_fusion.2), kind=kOutput, calls=%fused_computation.16 | convolution fusion | flops 5048893440 | bytes 33095680 | tf_op jit(solution)/shard_map/dot_general | solution.py:58
  278.5 7.3 %convolution_convert_fusion.5 = bf16[2560,960]{0,1:T(8,128)(2,1)} fusion(bf16[1024,960]{0,1:T(8,128)(2,1)S(1)} %copy-done.32, bf16[1024,2560]{1,0:T(8,128)(2,1)S(1)} %get-tuple-element.152), kind=kOutput, calls=%fused_computation.35 | convolution fusion | flops 5035622400 | bytes 12124160 | tf_op jit(solution)/shard_map/dot_general | solution.py:62
  285.9 7.8 %copy.205 = bf16[2560,960]{1,0:T(8,128)(2,1)} copy(bf16[2560,960]{0,1:T(8,128)(2,1)} %convolution_convert_fusion.5) | data formatting | bytes 9830400 | tf_op jit(solution)/shard_map/convert_element_type | solution.py:200
  297.4 18.2 %multiply_convert_fusion = (bf16[1024,2560]{1,0:T(8,128)(2,1)}, bf16[1024,2560]{1,0:T(8,128)(2,1)}) fusion(f32[1024,2560]{1,0:T(8,128)} %copy-done.70, f32[1024,2560]{1,0:T(8,128)} %get-tuple-element.153, bf16[1024,960]{0,1:T(8,128)(2,1)} %fusion.31, bf16[2560,960]{1,0:T(8,128)(2,1)} %bitcast.552), kind=kOutput, calls=%fused_computation.14 | convolution fusion | flops 5067243520 | bytes 38338560 | tf_op jit(solution)/shard_map/dot_general | solution.py:68
  321.1 8.4 %add_convert_fusion = bf16[1024,960]{0,1:T(8,128)(2,1)} fusion(f32[1024,960]{0,1:T(8,128)S(1)} %copy-done.1, bf16[1024,2560]{1,0:T(8,128)(2,1)} %copy-done.75, bf16[2560,960]{1,0:T(8,128)(2,1)S(1)} %bitcast.555), kind=kOutput, calls=%fused_computation.65 | convolution fusion | flops 5035130880 | bytes 16056320 | tf_op jit(solution)/shard_map/dot_general | solution.py:58
  334.5 6.1 convolution_convert_fusion.1
  340.7 6.1 convolution_convert_fusion
  346.8 17.3 %collective-permute-done.21 = bf16[8,1,80,960]{3,2,0,1:T(8,128)(2,1)S(1)} collective-permute-done((bf16[8,1,80,960]{3,2,0,1:T(8,128)(2,1)S(1)}, bf16[8,1,80,960]{3,2,0,1:T(8,128)(2,1)S(1)}, u32[]{:S(2)}, u32[]{:S(2)}) %collective-permute-start.21) | collective-permute-done | bytes 1228832 | tf_op jit(solution)/shard_map/ppermute | solution.py:82
  365.0 8.6 %fusion.153 = f32[1024,960]{0,1:T(8,128)} fusion(bf16[1024,2560]{1,0:T(8,128)(2,1)} %get-tuple-element.49, bf16[960,2560]{1,0:T(8,128)(2,1)S(1)} %bitcast.624), kind=kOutput, calls=%fused_computation.303 | convolution fusion | flops 5033164800 | bytes 14090240 | tf_op jit(solution)/shard_map/dot_general | solution.py:68
  377.5 10.4 %multiply_reduce_fusion = (f32[960]{0:T(1024)}, f32[1024]{0:T(1024)S(1)}, f32[1024,960]{0,1:T(8,128)S(1)}) fusion(f32[1024,960]{0,1:T(8,128)S(1)} %copy-done.1, f32[1024]{0:T(1024)S(1)} %add_rsqrt_fusion, f32[960]{0:T(1024)S(1)} %copy-done.52, f32[1024,960]{0,1:T(8,128)S(1)} %copy-done.74, bf16[1024,2560]{1,0:T(8,128)(2,1)} %get-tuple-element.50, ...), kind=kOutput, calls=%fused_computation.59 | convolution fusion | flops 5040044032 | bytes 21970432 | tf_op jit(solution)/shard_map/dot_general | solution.py:68
  393.7 7.9 %fusion.50 = bf16[1024,960]{0,1:T(8,128)(2,1)} fusion(bf16[1024,960]{0,1:T(8,128)(2,1)} %fusion.139, bf16[1024,960]{0,1:T(8,128)(2,1)} %bitcast.593, s32[1024]{0:T(1024)S(1)} %get-tuple-element.160, s32[1024]{0:T(1024)S(1)} %get-tuple-element.163, s32[1024]{0:T(1024)S(1)} %get-tuple-element.161, s32[1024]{0:T(1024)S(1)} %get-tuple-element.162, ...), kind=kOutput, calls=%fused_computation.116 | convolution fusion | flops 4035444736 | bytes 5916672 | tf_op jit(solution)/shard_map/dot_general | solution.py:62
  411.1 5.8 reshape.1040
  427.8 33.3 %fusion.3 = bf16[2,5,3,512,512]{3,4,2,1,0:T(8,128)(2,1)} fusion(bf16[2,512,5,3,64]{1,0,4,3,2:T(2,128)(2,1)} %reshape.1040, bf16[2,512,5,64,1]{1,0,3,2,4:T(2,128)(2,1)} %bitcast.609, f32[2,5,3,512,512]{3,4,2,1,0:T(8,128)} %get-tuple-element.149, f32[2,5,3,512]{3,2,1,0:T(4,128)S(1)} %copy-done.77), kind=kOutput, calls=%fused_computation.5 | convolution fusion | flops 2060467712 | bytes 49868800 | tf_op jit(solution)/shard_map/sub | solution.py:329
  461.1 13.1 %fusion.83 = bf16[2,512,5,64]{1,3,2,0:T(8,128)(2,1)S(1)} fusion(bf16[2,512,5,3,64]{1,0,4,3,2:T(2,128)(2,1)} %reshape.1040, f32[2,5,3,512,512]{3,4,2,1,0:T(8,128)} %get-tuple-element.149, f32[2,5,3,512]{3,2,1,0:T(4,128)S(1)} %copy-done.77), kind=kOutput, calls=%fused_computation.156 | convolution fusion | flops 1022689280 | bytes 34140160 | tf_op jit(solution)/shard_map/bgrst,bsgrd->btgd/dot_general | solution.py:327
  485.2 10.2 %multiply_bitcast_fusion = f32[2,512,5,3,64]{1,4,3,2,0:T(8,128)} fusion(bf16[2,5,3,512,512]{3,4,2,1,0:T(8,128)(2,1)} %fusion.3, bf16[2,512,5,32]{1,3,2,0:T(8,128)(2,1)S(1)} %bitcast.603, bf16[2,512,5,32]{1,3,2,0:T(8,128)(2,1)S(1)} %bitcast.605), kind=kOutput, calls=%fused_computation.60 | convolution fusion | flops 1008926720 | bytes 20316160 | tf_op jit(solution)/shard_map/bgrst,btgd->bsgrd/dot_general | solution.py:333
  495.5 11.0 %fusion.72 = f32[2,512,5,64]{1,3,2,0:T(8,128)S(1)} fusion(bf16[2,512,5,3,64]{1,4,3,2,0:T(8,128)(2,1)} %copy_dynamic-update-slice_fusion, bf16[2,5,3,512,512]{3,4,2,1,0:T(8,128)(2,1)} %fusion.3), kind=kOutput, calls=%fused_computation.130 | convolution fusion | flops 1006960640 | bytes 19005440 | tf_op jit(solution)/shard_map/bgrst,bsgrd->btgd/dot_general | solution.py:337
  527.7 8.9 %collective-permute-done.31 = bf16[4,1,32,2560]{3,2,0,1:T(8,128)(2,1)} collective-permute-done((bf16[4,1,32,2560]{3,2,0,1:T(8,128)(2,1)}, bf16[4,1,32,2560]{3,2,0,1:T(8,128)(2,1)}, u32[]{:S(2)}, u32[]{:S(2)}) %collective-permute-start.31) | collective-permute-done | bytes 655392 | tf_op jit(solution)/shard_map/ppermute | solution.py:82
  548.2 6.5 reshape.1061
  572.4 9.6 %convolution_convert_fusion.6 = bf16[1024,1600]{0,1:T(8,128)(2,1)} fusion(bf16[1024,1600]{0,1:T(8,128)(2,1)} %pad_maximum_fusion.4, bf16[1024,960]{0,1:T(8,128)(2,1)S(1)} %copy-done.15, f32[960]{0:T(1024)} %param.22, f32[1024]{0:T(1024)S(1)} %copy-done.56, s32[1024]{0:T(1024)S(1)} %copy-done.58, s32[1024]{0:T(1024)} %copy-done.63, s32[1024]{0:T(1024)S(1)} %copy-done.60, ...), kind=kOutput, calls=%fused_computation.69 | convolution fusion | flops 5382209536 | bytes 8546048 | tf_op jit(solution)/shard_map/dot_general | solution.py:62
  588.0 7.4 %fusion.30 = (f32[960]{0:T(1024)S(1)}, f32[1024]{0:T(1024)S(1)}, f32[1024,960]{0,1:T(8,128)S(1)}) fusion(bf16[1024,960]{0,1:T(8,128)(2,1)S(1)} %copy-done.16, f32[1024]{0:T(1024)S(1)} %copy-done.56, f32[960]{0:T(1024)S(1)} %copy-done.65, bf16[1024,1600]{0,1:T(8,128)(2,1)} %pad_maximum_fusion.4, bf16[960,2560]{1,0:T(8,128)(2,1)} %copy-done.71), kind=kOutput, calls=%fused_computation.58 | convolution fusion | flops 3152607232 | bytes 12385792 | tf_op jit(solution)/shard_map/dot_general | solution.py:68
  619.4 11.7 %collective-permute-done.37 = bf16[8,1,32,1600]{3,2,0,1:T(8,128)(2,1)S(1)} collective-permute-done((bf16[8,1,32,1600]{3,2,0,1:T(8,128)(2,1)S(1)}, bf16[8,1,32,1600]{3,2,0,1:T(8,128)(2,1)S(1)}, u32[]{:S(2)}, u32[]{:S(2)}) %collective-permute-start.37) | collective-permute-done | bytes 819232 | tf_op jit(solution)/shard_map/ppermute | solution.py:82
  631.9 7.7 %collective-permute-done.38 = bf16[4,1,32,1600]{3,2,0,1:T(8,128)(2,1)S(1)} collective-permute-done((bf16[4,1,32,1600]{3,2,0,1:T(8,128)(2,1)S(1)}, bf16[4,1,32,1600]{3,2,0,1:T(8,128)(2,1)S(1)}, u32[]{:S(2)}, u32[]{:S(2)}) %collective-permute-start.38) | collective-permute-done | bytes 409632 | tf_op jit(solution)/shard_map/ppermute | solution.py:82
  641.6 7.2 %collective-permute-done.39 = bf16[1,2,32,1600]{3,2,1,0:T(8,128)(2,1)S(1)} collective-permute-done((bf16[1,2,32,1600]{3,2,1,0:T(8,128)(2,1)S(1)}, bf16[1,2,32,1600]{3,2,1,0:T(8,128)(2,1)S(1)}, u32[]{:S(2)}, u32[]{:S(2)}) %collective-permute-start.39) | collective-permute-done | bytes 204832 | tf_op jit(solution)/shard_map/ppermute | solution.py:82
  (457 shorter events, 268.8 us)
Async XLA Ops:
  5.5 21.9 %collective-permute-start = (bf16[1,32,2560]{2,1,0:T(8,128)(2,1)}, bf16[1,32,2560]{2,1,0:T(8,128)(2,1)}, u32[]{:S(2)}, u32[]{:S(2)}) collective-permute-start(bf16[1,32,2560]{2,1,0:T(8,128)(2,1)} %pad_bitcast_fusion.2), channel_id=1, source_target_pairs={{0,8},{1,9},{2,10},{3,11},{4,12},{5,13},{6,14},{7,15},{8,0},{9,1},... | collective-permute-start | bytes 491528 | tf_op jit(solution)/shard_map/ppermute | solution.py:82
  10.4 18.2 %collective-permute-start.10 = (bf16[1,32,2560]{2,1,0:T(8,128)(2,1)}, bf16[1,32,2560]{2,1,0:T(8,128)(2,1)S(1)}, u32[]{:S(2)}, u32[]{:S(2)}) collective-permute-start(bf16[1,32,2560]{2,1,0:T(8,128)(2,1)} %pad_bitcast_fusion), channel_id=1, source_target_pairs={{0,8},{1,9},{2,10},{3,11},{4,12},{5,13},{6,14},{7,15},{8,0},{9,1},... | collective-permute-start | bytes 491528 | tf_op jit(solution)/shard_map/ppermute | solution.py:82
  24.6 39.0 %collective-permute-start.16 = (bf16[2,80,960]{2,1,0:T(8,128)(2,1)S(1)}, bf16[2,80,960]{2,1,0:T(8,128)(2,1)S(1)}, u32[]{:S(2)}, u32[]{:S(2)}) collective-permute-start(bf16[2,80,960]{2,1,0:T(8,128)(2,1)S(1)} %maximum_bitcast_fusion.4), channel_id=1, source_target_pairs={{0,16},{1,17},{2,18},{3,19},{4,20},{5,21},{6,22},{7,23},{8,24},{9,... | collective-permute-start | bytes 921608 | tf_op jit(solution)/shard_map/ppermute | solution.py:82
  28.4 42.1 %collective-permute-start.1 = (bf16[2,32,2560]{2,1,0:T(8,128)(2,1)S(1)}, bf16[2,32,2560]{2,1,0:T(8,128)(2,1)S(1)}, u32[]{:S(2)}, u32[]{:S(2)}) collective-permute-start(bf16[2,32,2560]{2,1,0:T(8,128)(2,1)S(1)} %maximum_bitcast_fusion.1), channel_id=1, source_target_pairs={{0,16},{1,17},{2,18},{3,19},{4,20},{5,21},{6,22},{7,23},{8,24},{9,... | collective-permute-start | bytes 983048 | tf_op jit(solution)/shard_map/ppermute | solution.py:82
  29.7 47.9 %collective-permute-start.6 = (bf16[2,32,2560]{2,1,0:T(8,128)(2,1)S(1)}, bf16[2,32,2560]{2,1,0:T(8,128)(2,1)S(1)}, u32[]{:S(2)}, u32[]{:S(2)}) collective-permute-start(bf16[2,32,2560]{2,1,0:T(8,128)(2,1)S(1)} %maximum_bitcast_fusion.2), channel_id=1, source_target_pairs={{0,16},{1,17},{2,18},{3,19},{4,20},{5,21},{6,22},{7,23},{8,24},{9,... | collective-permute-start | bytes 983048 | tf_op jit(solution)/shard_map/ppermute | solution.py:82
  32.6 50.8 %collective-permute-start.11 = (bf16[2,32,2560]{2,1,0:T(8,128)(2,1)S(1)}, bf16[2,32,2560]{2,1,0:T(8,128)(2,1)S(1)}, u32[]{:S(2)}, u32[]{:S(2)}) collective-permute-start(bf16[2,32,2560]{2,1,0:T(8,128)(2,1)S(1)} %maximum_bitcast_fusion.3), channel_id=1, source_target_pairs={{0,16},{1,17},{2,18},{3,19},{4,20},{5,21},{6,22},{7,23},{8,24},{9,... | collective-permute-start | bytes 983048 | tf_op jit(solution)/shard_map/ppermute | solution.py:82
  63.6 21.5 %collective-permute-start.17 = (bf16[4,80,960]{2,1,0:T(8,128)(2,1)S(1)}, bf16[4,80,960]{2,1,0:T(8,128)(2,1)S(1)}, u32[]{:S(2)}, u32[]{:S(2)}) collective-permute-start(bf16[4,80,960]{2,1,0:T(8,128)(2,1)S(1)} %bitcast.586), channel_id=1, source_target_pairs={{0,4},{1,5},{2,6},{3,7},{4,0},{5,1},{6,2},{7,3},{8,12},{9,13},{10,... | collective-permute-start | bytes 1843208 | tf_op jit(solution)/shard_map/ppermute | solution.py:82
  85.4 43.9 %collective-permute-start.18 = (bf16[8,80,960]{2,1,0:T(8,128)(2,1)S(1)}, bf16[8,80,960]{2,1,0:T(8,128)(2,1)S(1)}, u32[]{:S(2)}, u32[]{:S(2)}) collective-permute-start(bf16[8,80,960]{2,1,0:T(8,128)(2,1)S(1)} %bitcast.572), channel_id=1, source_target_pairs={{0,2},{1,3},{2,0},{3,1},{4,6},{5,7},{6,4},{7,5},{8,10},{9,11},{10,... | collective-permute-start | bytes 3686408 | tf_op jit(solution)/shard_map/ppermute | solution.py:82
  86.2 43.7 %collective-permute-start.3 = (bf16[8,32,2560]{2,1,0:T(8,128)(2,1)S(1)}, bf16[8,32,2560]{2,1,0:T(8,128)(2,1)S(1)}, u32[]{:S(2)}, u32[]{:S(2)}) collective-permute-start(bf16[8,32,2560]{2,1,0:T(8,128)(2,1)S(1)} %bitcast.599), channel_id=1, source_target_pairs={{0,4},{1,5},{2,6},{3,7},{4,0},{5,1},{6,2},{7,3},{8,12},{9,13},{10,... | collective-permute-start | bytes 3932168 | tf_op jit(solution)/shard_map/ppermute | solution.py:82
  95.8 59.5 %collective-permute-start.8 = (bf16[8,32,2560]{2,1,0:T(8,128)(2,1)S(1)}, bf16[8,32,2560]{2,1,0:T(8,128)(2,1)S(1)}, u32[]{:S(2)}, u32[]{:S(2)}) collective-permute-start(bf16[8,32,2560]{2,1,0:T(8,128)(2,1)S(1)} %bitcast.571), channel_id=1, source_target_pairs={{0,2},{1,3},{2,0},{3,1},{4,6},{5,7},{6,4},{7,5},{8,10},{9,11},{10,... | collective-permute-start | bytes 3932168 | tf_op jit(solution)/shard_map/ppermute | solution.py:82
  101.5 55.8 %collective-permute-start.13 = (bf16[8,32,2560]{2,1,0:T(8,128)(2,1)S(1)}, bf16[8,32,2560]{2,1,0:T(8,128)(2,1)S(1)}, u32[]{:S(2)}, u32[]{:S(2)}) collective-permute-start(bf16[8,32,2560]{2,1,0:T(8,128)(2,1)S(1)} %bitcast.598), channel_id=1, source_target_pairs={{0,4},{1,5},{2,6},{3,7},{4,0},{5,1},{6,2},{7,3},{8,12},{9,13},{10,... | collective-permute-start | bytes 3932168 | tf_op jit(solution)/shard_map/ppermute | solution.py:82
  129.9 28.6 %collective-permute-start.19 = (bf16[16,80,960]{2,1,0:T(8,128)(2,1)S(1)}, bf16[16,80,960]{2,1,0:T(8,128)(2,1)S(1)}, u32[]{:S(2)}, u32[]{:S(2)}) collective-permute-start(bf16[16,80,960]{2,1,0:T(8,128)(2,1)S(1)} %bitcast.543), channel_id=1, source_target_pairs={{0,1},{1,0},{2,3},{3,2},{4,5},{5,4},{6,7},{7,6},{8,9},{9,8},{10,11... | collective-permute-start | bytes 7372808 | tf_op jit(solution)/shard_map/ppermute | solution.py:82
  130.6 31.2 %collective-permute-start.4 = (bf16[16,32,2560]{2,1,0:T(8,128)(2,1)S(1)}, bf16[16,32,2560]{2,1,0:T(8,128)(2,1)S(1)}, u32[]{:S(2)}, u32[]{:S(2)}) collective-permute-start(bf16[16,32,2560]{2,1,0:T(8,128)(2,1)S(1)} %bitcast.544), channel_id=1, source_target_pairs={{0,1},{1,0},{2,3},{3,2},{4,5},{5,4},{6,7},{7,6},{8,9},{9,8},{10,11... | collective-permute-start | bytes 7864328 | tf_op jit(solution)/shard_map/ppermute | solution.py:82
  157.3 67.1 %collective-permute-start.9 = (bf16[16,32,2560]{2,1,0:T(8,128)(2,1)}, bf16[16,32,2560]{2,1,0:T(8,128)(2,1)}, u32[]{:S(2)}, u32[]{:S(2)}) collective-permute-start(bf16[16,32,2560]{2,1,0:T(8,128)(2,1)} %bitcast.42), channel_id=1, source_target_pairs={{0,1},{1,0},{2,3},{3,2},{4,5},{5,4},{6,7},{7,6},{8,9},{9,8},{10,11... | collective-permute-start | bytes 7864328 | tf_op jit(solution)/shard_map/ppermute | solution.py:82
  157.9 85.7 %collective-permute-start.14 = (bf16[16,32,2560]{2,1,0:T(8,128)(2,1)S(1)}, bf16[16,32,2560]{2,1,0:T(8,128)(2,1)}, u32[]{:S(2)}, u32[]{:S(2)}) collective-permute-start(bf16[16,32,2560]{2,1,0:T(8,128)(2,1)S(1)} %bitcast.542), channel_id=1, source_target_pairs={{0,1},{1,0},{2,3},{3,2},{4,5},{5,4},{6,7},{7,6},{8,9},{9,8},{10,11... | collective-permute-start | bytes 7864328 | tf_op jit(solution)/shard_map/ppermute | solution.py:82
  297.4 32.2 %collective-permute-start.20 = (bf16[16,1,80,960]{3,2,0,1:T(8,128)(2,1)}, bf16[16,1,80,960]{3,2,0,1:T(8,128)(2,1)}, u32[]{:S(2)}, u32[]{:S(2)}) collective-permute-start(bf16[16,1,80,960]{3,2,0,1:T(8,128)(2,1)} %dynamic-slice_bitcast_fusion.2), channel_id=1, source_target_pairs={{0,1},{1,0},{2,3},{3,2},{4,5},{5,4},{6,7},{7,6},{8,9},{9,8},{10,11... | collective-permute-start | bytes 7372808 | tf_op jit(solution)/shard_map/ppermute | solution.py:82
  332.9 31.2 %collective-permute-start.21 = (bf16[8,1,80,960]{3,2,0,1:T(8,128)(2,1)S(1)}, bf16[8,1,80,960]{3,2,0,1:T(8,128)(2,1)S(1)}, u32[]{:S(2)}, u32[]{:S(2)}) collective-permute-start(bf16[8,1,80,960]{3,2,0,1:T(8,128)(2,1)S(1)} %dynamic-slice_bitcast_fusion.6), channel_id=1, source_target_pairs={{0,2},{1,3},{2,0},{3,1},{4,6},{5,7},{6,4},{7,5},{8,10},{9,11},{10,... | collective-permute-start | bytes 3686408 | tf_op jit(solution)/shard_map/ppermute | solution.py:82
  364.9 27.9 %collective-permute-start.22 = (bf16[16,1,32,2560]{3,2,0,1:T(8,128)(2,1)S(1)}, bf16[16,1,32,2560]{3,2,0,1:T(8,128)(2,1)S(1)}, u32[]{:S(2)}, u32[]{:S(2)}) collective-permute-start(bf16[16,1,32,2560]{3,2,0,1:T(8,128)(2,1)S(1)} %dynamic-slice_bitcast_fusion.1), channel_id=1, source_target_pairs={{0,1},{1,0},{2,3},{3,2},{4,5},{5,4},{6,7},{7,6},{8,9},{9,8},{10,11... | collective-permute-start | bytes 7864328 | tf_op jit(solution)/shard_map/ppermute | solution.py:82
  375.3 41.6 %collective-permute-start.23 = (bf16[16,1,32,2560]{3,2,0,1:T(8,128)(2,1)}, bf16[16,1,32,2560]{3,2,0,1:T(8,128)(2,1)}, u32[]{:S(2)}, u32[]{:S(2)}) collective-permute-start(bf16[16,1,32,2560]{3,2,0,1:T(8,128)(2,1)} %dynamic-slice_bitcast_fusion), channel_id=1, source_target_pairs={{0,1},{1,0},{2,3},{3,2},{4,5},{5,4},{6,7},{7,6},{8,9},{9,8},{10,11... | collective-permute-start | bytes 7864328 | tf_op jit(solution)/shard_map/ppermute | solution.py:82
  421.5 55.4 %collective-permute-start.25 = (bf16[16,1,32,960]{3,2,0,1:T(8,128)(2,1)}, bf16[16,1,32,960]{3,2,0,1:T(8,128)(2,1)}, u32[]{:S(2)}, u32[]{:S(2)}) collective-permute-start(bf16[16,1,32,960]{3,2,0,1:T(8,128)(2,1)} %dynamic-slice_bitcast_fusion.7), channel_id=1, source_target_pairs={{0,1},{1,0},{2,3},{3,2},{4,5},{5,4},{6,7},{7,6},{8,9},{9,8},{10,11... | collective-permute-start | bytes 2949128 | tf_op jit(solution)/shard_map/ppermute | solution.py:82
  422.7 57.0 %collective-permute-start.26 = (bf16[4,2,32,2560]{3,2,1,0:T(8,128)(2,1)}, bf16[4,2,32,2560]{3,2,1,0:T(8,128)(2,1)}, u32[]{:S(2)}, u32[]{:S(2)}) collective-permute-start(bf16[4,2,32,2560]{3,2,1,0:T(8,128)(2,1)} %dynamic-slice_bitcast_fusion.5), channel_id=1, source_target_pairs={{0,4},{1,5},{2,6},{3,7},{4,0},{5,1},{6,2},{7,3},{8,12},{9,13},{10,... | collective-permute-start | bytes 3932168 | tf_op jit(solution)/shard_map/ppermute | solution.py:82
  425.6 56.9 %collective-permute-start.27 = (bf16[8,1,32,2560]{3,2,0,1:T(8,128)(2,1)}, bf16[8,1,32,2560]{3,2,0,1:T(8,128)(2,1)}, u32[]{:S(2)}, u32[]{:S(2)}) collective-permute-start(bf16[8,1,32,2560]{3,2,0,1:T(8,128)(2,1)} %dynamic-slice_bitcast_fusion.4), channel_id=1, source_target_pairs={{0,2},{1,3},{2,0},{3,1},{4,6},{5,7},{6,4},{7,5},{8,10},{9,11},{10,... | collective-permute-start | bytes 3932168 | tf_op jit(solution)/shard_map/ppermute | solution.py:82
  427.8 47.2 %collective-permute-start.28 = (bf16[1,2,80,960]{3,2,1,0:T(8,128)(2,1)}, bf16[1,2,80,960]{3,2,1,0:T(8,128)(2,1)}, u32[]{:S(2)}, u32[]{:S(2)}) collective-permute-start(bf16[1,2,80,960]{3,2,1,0:T(8,128)(2,1)} %dynamic-slice_bitcast_fusion.16), channel_id=1, source_target_pairs={{0,16},{1,17},{2,18},{3,19},{4,20},{5,21},{6,22},{7,23},{8,24},{9,... | collective-permute-start | bytes 921608 | tf_op jit(solution)/shard_map/ppermute | solution.py:82
  518.4 18.1 %collective-permute-start.31 = (bf16[4,1,32,2560]{3,2,0,1:T(8,128)(2,1)}, bf16[4,1,32,2560]{3,2,0,1:T(8,128)(2,1)}, u32[]{:S(2)}, u32[]{:S(2)}) collective-permute-start(bf16[4,1,32,2560]{3,2,0,1:T(8,128)(2,1)} %dynamic-slice_bitcast_fusion.9), channel_id=1, source_target_pairs={{0,4},{1,5},{2,6},{3,7},{4,0},{5,1},{6,2},{7,3},{8,12},{9,13},{10,... | collective-permute-start | bytes 1966088 | tf_op jit(solution)/shard_map/ppermute | solution.py:82
  537.8 21.9 %collective-permute-start.32 = (bf16[4,1,32,960]{3,2,0,1:T(8,128)(2,1)S(1)}, bf16[4,1,32,960]{3,2,0,1:T(8,128)(2,1)}, u32[]{:S(2)}, u32[]{:S(2)}) collective-permute-start(bf16[4,1,32,960]{3,2,0,1:T(8,128)(2,1)S(1)} %dynamic-slice_bitcast_fusion.17), channel_id=1, source_target_pairs={{0,2},{1,3},{2,0},{3,1},{4,6},{5,7},{6,4},{7,5},{8,10},{9,11},{10,... | collective-permute-start | bytes 737288 | tf_op jit(solution)/shard_map/ppermute | solution.py:82
  539.2 25.9 %collective-permute-start.33 = (bf16[1,2,32,2560]{3,2,1,0:T(8,128)(2,1)}, bf16[1,2,32,2560]{3,2,1,0:T(8,128)(2,1)}, u32[]{:S(2)}, u32[]{:S(2)}) collective-permute-start(bf16[1,2,32,2560]{3,2,1,0:T(8,128)(2,1)} %dynamic-slice_bitcast_fusion.15), channel_id=1, source_target_pairs={{0,16},{1,17},{2,18},{3,19},{4,20},{5,21},{6,22},{7,23},{8,24},{9,... | collective-permute-start | bytes 983048 | tf_op jit(solution)/shard_map/ppermute | solution.py:82
  542.6 27.3 %collective-permute-start.34 = (bf16[1,2,32,2560]{3,2,1,0:T(8,128)(2,1)}, bf16[1,2,32,2560]{3,2,1,0:T(8,128)(2,1)}, u32[]{:S(2)}, u32[]{:S(2)}) collective-permute-start(bf16[1,2,32,2560]{3,2,1,0:T(8,128)(2,1)} %dynamic-slice_bitcast_fusion.14), channel_id=1, source_target_pairs={{0,16},{1,17},{2,18},{3,19},{4,20},{5,21},{6,22},{7,23},{8,24},{9,... | collective-permute-start | bytes 983048 | tf_op jit(solution)/shard_map/ppermute | solution.py:82
  587.6 24.9 %collective-permute-start.36 = (bf16[16,1,32,1600]{3,2,0,1:T(8,128)(2,1)S(1)}, bf16[16,1,32,1600]{3,2,0,1:T(8,128)(2,1)S(1)}, u32[]{:S(2)}, u32[]{:S(2)}) collective-permute-start(bf16[16,1,32,1600]{3,2,0,1:T(8,128)(2,1)S(1)} %dynamic-slice_bitcast_fusion.3), channel_id=1, source_target_pairs={{0,1},{1,0},{2,3},{3,2},{4,5},{5,4},{6,7},{7,6},{8,9},{9,8},{10,11... | collective-permute-start | bytes 4915208 | tf_op jit(solution)/shard_map/ppermute | solution.py:82
  595.7 36.1 %collective-permute-start.42 = (bf16[1,1,32,2560]{3,2,1,0:T(8,128)(2,1)S(1)}, bf16[1,1,32,2560]{3,2,1,0:T(8,128)(2,1)S(1)}, u32[]{:S(2)}, u32[]{:S(2)}) collective-permute-start(bf16[1,1,32,2560]{3,2,1,0:T(8,128)(2,1)S(1)} %get-tuple-element.127), channel_id=1, source_target_pairs={{0,8},{1,9},{2,10},{3,11},{4,12},{5,13},{6,14},{7,15},{8,0},{9,1},... | collective-permute-start | bytes 491528 | tf_op jit(solution)/shard_map/ppermute | solution.py:82
  600.1 40.0 %collective-permute-start.43 = (bf16[1,1,32,2560]{3,2,1,0:T(8,128)(2,1)S(1)}, bf16[1,1,32,2560]{3,2,1,0:T(8,128)(2,1)S(1)}, u32[]{:S(2)}, u32[]{:S(2)}) collective-permute-start(bf16[1,1,32,2560]{3,2,1,0:T(8,128)(2,1)S(1)} %get-tuple-element.125), channel_id=1, source_target_pairs={{0,8},{1,9},{2,10},{3,11},{4,12},{5,13},{6,14},{7,15},{8,0},{9,1},... | collective-permute-start | bytes 491528 | tf_op jit(solution)/shard_map/ppermute | solution.py:82
  607.1 41.9 %collective-permute-start.41 = (bf16[1,1,32,960]{3,2,1,0:T(8,128)(2,1)S(1)}, bf16[1,1,32,960]{3,2,1,0:T(8,128)(2,1)}, u32[]{:S(2)}, u32[]{:S(2)}) collective-permute-start(bf16[1,1,32,960]{3,2,1,0:T(8,128)(2,1)S(1)} %get-tuple-element.139), channel_id=1, source_target_pairs={{0,8},{1,9},{2,10},{3,11},{4,12},{5,13},{6,14},{7,15},{8,0},{9,1},... | collective-permute-start | bytes 184328 | tf_op jit(solution)/shard_map/ppermute | solution.py:82
  613.1 18.0 %collective-permute-start.37 = (bf16[8,1,32,1600]{3,2,0,1:T(8,128)(2,1)S(1)}, bf16[8,1,32,1600]{3,2,0,1:T(8,128)(2,1)S(1)}, u32[]{:S(2)}, u32[]{:S(2)}) collective-permute-start(bf16[8,1,32,1600]{3,2,0,1:T(8,128)(2,1)S(1)} %dynamic-slice_bitcast_fusion.8), channel_id=1, source_target_pairs={{0,2},{1,3},{2,0},{3,1},{4,6},{5,7},{6,4},{7,5},{8,10},{9,11},{10,... | collective-permute-start | bytes 2457608 | tf_op jit(solution)/shard_map/ppermute | solution.py:82
  (106 other events, 3418.3 us)

commit v3 on v2

--- a/solution.py
+++ b/solution.py
@@ -86,10 +86,17 @@
     return (lax.axis_index("dp") >> bit) & 1
 
 
-def gather_rows(shard, order):
-    current = shard[None]
-    held = []
-    for bit in order:
+class Doubling:
+    def __init__(self, shard, order):
+        self.current = shard[None]
+        self.order = list(order)
+        self.held = []
+
+    def step(self):
+        if not self.order:
+            return
+        bit = self.order.pop(0)
+        current, held = self.current, self.held
         other = swap(current, bit)
         place = sum(1 for b in held if b > bit)
         shape = current.shape
@@ -100,7 +107,16 @@
         high = jnp.where(upper, mine, theirs)
         current = jnp.concatenate([low, high], axis=1).reshape((shape[0] * 2,) + shape[1:])
         held.append(bit)
-    return current
+        self.current = current
+
+    def finish(self):
+        while self.order:
+            self.step()
+        return self.current
+
+
+def gather_rows(shard, order):
+    return Doubling(shard, order).finish()
 
 
 class Halving:
@@ -133,6 +149,8 @@
 
 
 def advance(chains, *values):
+    if not chains:
+        return values if len(values) > 1 else values[0]
     held, values = lax.optimization_barrier((tuple(c.current for c in chains), values))
     for chain, current in zip(chains, held):
         chain.current = current
@@ -259,17 +277,21 @@
             axis=1,
         )
         mat_out = gather_matrix(w_out, D, False)
+    late = []
     if aligned:
-        mat_gate = gather_padded(w_gate.reshape(-1, FF), chosen, True)
-        mat_up = gather_padded(w_up.reshape(-1, FF), chosen, False)
-    else:
-        mat_gate = gather_matrix(w_gate, FF, True)
-        mat_up = gather_matrix(w_up, FF, False)
+        pad = padded(height) - height
+        late = [
+            Doubling(
+                jnp.pad(flat.reshape(-1, FF).astype(jnp.bfloat16), ((0, pad), (0, 0))),
+                gather_order(flip),
+            )
+            for flat, flip in ((w_gate, True), (w_up, False))
+        ]
+        late.append(Doubling(w_down.reshape(-1, D).astype(jnp.bfloat16), gather_order(True)))
+        mat_qkv, mat_out = advance(late, mat_qkv, mat_out)
 
     def widen(value):
         return matmul(value, chosen).astype(jnp.bfloat16) if aligned else value
-
-    mat_down = gather_matrix(w_down, D, True)
 
     allowed, placed, living = jax.vmap(block_mask)(position.reshape(blocks, slots))
     cosines, sines = rotary_tables(placed.reshape(-1), HD)
@@ -278,6 +300,7 @@
     factor_one = lax.rsqrt(jnp.mean(inputs * inputs, axis=-1, keepdims=True) + EPS)
     normed = (inputs * factor_one * gain_attn).astype(jnp.bfloat16)
     qkv = matmul(normed, mat_qkv)
+    qkv = advance(late, qkv)
     query = qkv[:, :D].reshape(rows, H, HD)
     keys = qkv[:, D : D + kvw].reshape(rows, KV, HD)
     values = qkv[:, D + kvw :].astype(jnp.bfloat16).reshape(blocks, slots, KV, HD)
@@ -285,14 +308,26 @@
         rotate(query, cosines, sines).astype(jnp.bfloat16).reshape(blocks, slots, KV, groups, HD)
     )
     keys_rot = rotate(keys, cosines, sines).astype(jnp.bfloat16).reshape(blocks, slots, KV, HD)
+    query_rot, keys_rot = advance(late, query_rot, keys_rot)
     scores = attend(query_rot, keys_rot, values, allowed, scale)
     top = jnp.max(scores, axis=-1, keepdims=True)
     expd = jnp.exp(scores - top)
     total_exp = jnp.sum(expd, axis=-1, keepdims=True)
     probs = (expd / total_exp).astype(jnp.bfloat16)
+    probs = advance(late, probs)
     mixed = jnp.einsum("bgrst,btgd->bsgrd", probs, values, preferred_element_type=jnp.float32)
     mixed = mixed.reshape(rows, D).astype(jnp.bfloat16)
+    mixed = advance(late, mixed)
     resid = inputs + matmul(mixed, mat_out)
+    if aligned:
+        wide_gate, wide_up, wide_down = [c.finish() for c in late]
+        mat_gate = matmul(chosen, wide_gate.reshape(-1, FF)).astype(jnp.bfloat16)
+        mat_up = matmul(chosen, wide_up.reshape(-1, FF)).astype(jnp.bfloat16)
+        mat_down = wide_down.reshape(-1, D)
+    else:
+        mat_gate = gather_matrix(w_gate, FF, True)
+        mat_up = gather_matrix(w_up, FF, False)
+        mat_down = gather_matrix(w_down, D, True)
     factor_two = lax.rsqrt(jnp.mean(resid * resid, axis=-1, keepdims=True) + EPS)
     normed_two = (resid * factor_two * gain_mlp).astype(jnp.bfloat16)
     wide_two = widen(normed_two)

time: 667 us -> 691 us (1.036)
  waiting for transfers between devices: 183 us -> 200 us
  other arithmetic: 79.7 us -> 90.9 us
  matrix products: 248 us -> 238 us
    div x0 -> x1, matrix products: none -> 24.4 us  [body(): probs = (expd / total_exp).astype(jnp.bfloat16)]
    sub x1 -> x0, matrix products: 17.7 us -> none  [body(): expd = jnp.exp(scores - top)]
    ppermute x50, waiting for transfers between devices: 183 us -> 200 us  [swap(): return lax.ppermute(value, 'dp', [(i, i ^ 1 << bit) for i in range(owners)])]
    select_n x19 -> x20, other arithmetic: 10.5 us -> 19.4 us  [step(): low = jnp.where(upper, theirs, mine)]
  transfers between devices with their start and end apart: 50 -> 50, of which waited for: 23 -> 23; matrix products, arithmetic and copies ran while one was open for 48% -> 46% of each run, Pallas kernels for 0% -> 0%
where the time goes in v3:
time: 691 us; the launch traced here: 683 us
  matrix products  238 us (34%)
  waiting for transfers between devices  200 us (29%)
  local copies, waits for them, and re-layouts  91.4 us (13%)
  other arithmetic  90.9 us (13%)
  starting transfers between devices  59.4 us (9%)
    ppermute x50, waiting for transfers between devices, swap(): return lax.ppermute(value, 'dp', [(i, i ^ 1 << bit) for i in range(owners)])  200 us
    dot_general x9, matrix products, matmul(): return jnp.dot(first, second, preferred_element_type=jnp.float32)  61.9 us
    ppermute x50, starting transfers between devices, swap(): return lax.ppermute(value, 'dp', [(i, i ^ 1 << bit) for i in range(owners)])  59.4 us
    dot_general x5, matrix products, right_contract(): lax.dot_general(first, second, (((1,), (1,)), ((), ())), preferred_elemen...  49.4 us
    dot_general x5, matrix products, left_contract(): lax.dot_general(first, second, (((0,), (0,)), ((), ())), preferred_elemen...  36.2 us
    sub x1, matrix products, body(): d_probs - jnp.sum(probs_back * d_probs, axis=-1, keepdims=True)  27.5 us
    div x1, matrix products, body(): probs = (expd / total_exp).astype(jnp.bfloat16)  24.4 us
    reshape x14, other arithmetic, step(): self.current = total.reshape((shape[0] // 2,) + shape[1:])  23.9 us
  transfers between devices with their start and end apart: 50, of which 23 were waited for; matrix products, arithmetic and copies ran while one was open for 46% of the time, Pallas kernels for 0%

profile of v3, /device:TPU:0, one launch (start us, length us, event | category | flops | bytes accessed | tf_op | source)
XLA Modules:
  0.0 683.0 jit_solution(11023316248130469488)
XLA Ops:
  14.8 14.1 %collective-permute-done.1 = bf16[2,32,2560]{2,1,0:T(8,128)(2,1)S(1)} collective-permute-done((bf16[2,32,2560]{2,1,0:T(8,128)(2,1)S(1)}, bf16[2,32,2560]{2,1,0:T(8,128)(2,1)S(1)}, u32[]{:S(2)}, u32[]{:S(2)}) %collective-permute-start.1) | collective-permute-done | bytes 327712 | tf_op jit(solution)/shard_map/ppermute | solution.py:82
  30.4 14.4 %collective-permute-done.2 = bf16[4,32,2560]{2,1,0:T(8,128)(2,1)S(1)} collective-permute-done((bf16[4,32,2560]{2,1,0:T(8,128)(2,1)S(1)}, bf16[4,32,2560]{2,1,0:T(8,128)(2,1)S(1)}, u32[]{:S(2)}, u32[]{:S(2)}) %collective-permute-start.2) | collective-permute-done | bytes 655392 | tf_op jit(solution)/shard_map/ppermute | solution.py:82
  48.7 25.5 %collective-permute-done.3 = bf16[8,32,2560]{2,1,0:T(8,128)(2,1)} collective-permute-done((bf16[8,32,2560]{2,1,0:T(8,128)(2,1)S(1)}, bf16[8,32,2560]{2,1,0:T(8,128)(2,1)}, u32[]{:S(2)}, u32[]{:S(2)}) %collective-permute-start.3) | collective-permute-done | bytes 1310752 | tf_op jit(solution)/shard_map/ppermute | solution.py:82
  129.9 26.9 %collective-permute-done.10 = bf16[2,80,960]{2,1,0:T(8,128)(2,1)} collective-permute-done((bf16[2,80,960]{2,1,0:T(8,128)(2,1)}, bf16[2,80,960]{2,1,0:T(8,128)(2,1)}, u32[]{:S(2)}, u32[]{:S(2)}) %collective-permute-start.10) | collective-permute-done | bytes 307232 | tf_op jit(solution)/shard_map/ppermute | solution.py:82
  165.6 24.4 %fusion.148 = (bf16[2,5,3,512,512]{3,4,2,1,0:T(8,128)(2,1)}, f32[2,5,3,512,512]{3,4,2,1,0:T(8,128)}) fusion(pred[2,512,512]{1,2,0:T(8,128)(4,1)} %and_or_fusion, bf16[2,512,5,3,64]{1,0,4,3,2:T(2,128)(2,1)S(1)} %pad_maximum_fusion.9, bf16[2,512,5,64,1]{1,0,3,2,4:T(2,128)(2,1)S(1)} %bitcast.528), kind=kOutput, calls=%fused_computation.291 | convolution fusion | flops 1045986304 | bytes 50331648 | tf_op jit(solution)/shard_map/div | solution.py:316
  205.0 8.2 %convert_bitcast_fusion = bf16[2,512,5,3,64]{1,4,3,2,0:T(8,128)(2,1)S(1)} fusion(bf16[2,5,3,512,512]{3,4,2,1,0:T(8,128)(2,1)} %get-tuple-element.82, bf16[2,512,5,64,1]{1,0,3,2,4:T(2,128)(2,1)S(1)} %bitcast.477), kind=kOutput, calls=%fused_computation.105 | convolution fusion | flops 1007616000 | bytes 18350080 | tf_op jit(solution)/shard_map/bgrst,btgd->bsgrd/dot_general | solution.py:318
  217.1 12.7 %collective-permute-done.16 = bf16[8,80,960]{2,1,0:T(8,128)(2,1)} collective-permute-done((bf16[8,80,960]{2,1,0:T(8,128)(2,1)S(1)}, bf16[8,80,960]{2,1,0:T(8,128)(2,1)}, u32[]{:S(2)}, u32[]{:S(2)}) %collective-permute-start.16) | collective-permute-done | bytes 1228832 | tf_op jit(solution)/shard_map/ppermute | solution.py:82
  233.3 21.7 %collective-permute-done.14 = bf16[8,32,2560]{2,1,0:T(8,128)(2,1)S(1)} collective-permute-done((bf16[8,32,2560]{2,1,0:T(8,128)(2,1)}, bf16[8,32,2560]{2,1,0:T(8,128)(2,1)S(1)}, u32[]{:S(2)}, u32[]{:S(2)}) %collective-permute-start.14) | collective-permute-done | bytes 1310752 | tf_op jit(solution)/shard_map/ppermute | solution.py:82
  286.1 8.3 %fusion.159 = f32[1024,2560]{1,0:T(8,128)} fusion(bf16[1024,960]{0,1:T(8,128)(2,1)S(1)} %multiply_convert_fusion.3, bf16[960,2560]{1,0:T(8,128)(2,1)S(1)} %convolution_convert_fusion.3), kind=kOutput, calls=%fused_computation.292 | convolution fusion | flops 5033164800 | bytes 17367040 | tf_op jit(solution)/shard_map/dot_general | solution.py:58
  295.9 6.8 %convolution_convert_fusion.2 = bf16[960,2560]{1,0:T(8,128)(2,1)} fusion(bf16[1024,2560]{1,0:T(8,128)(2,1)S(1)} %bitcast.508, s32[1024]{0:T(1024)S(1)} %get-tuple-element.202, s32[1024]{0:T(1024)S(1)} %copy-done.72, s32[1024]{0:T(1024)S(1)} %get-tuple-element.203, s32[1024]{0:T(1024)S(1)} %get-tuple-element.204, pred[1024]{0:T(1024)(128)(4,1)S(1)} %copy-done.78, ...), kind=kOutput, calls=%fused_computation.29 | convolution fusion | flops 5042503680 | bytes 10176512 | tf_op jit(solution)/shard_map/dot_general | solution.py:58
  302.7 12.6 %multiply_convert_fusion.2 = (bf16[1024,2560]{1,0:T(8,128)(2,1)S(1)}, f32[1024,2560]{1,0:T(8,128)}) fusion(f32[1024,2560]{1,0:T(8,128)S(1)} %bitcast.563, bf16[1024,960]{0,1:T(8,128)(2,1)S(1)} %multiply_convert_fusion.3, bf16[960,2560]{1,0:T(8,128)(2,1)} %convolution_convert_fusion.2), kind=kOutput, calls=%fused_computation.17 | convolution fusion | flops 5048893440 | bytes 33095680 | tf_op jit(solution)/shard_map/dot_general | solution.py:58
  317.6 7.0 %convolution_convert_fusion.5 = bf16[2560,960]{0,1:T(8,128)(2,1)} fusion(bf16[1024,960]{0,1:T(8,128)(2,1)S(1)} %copy-done.41, bf16[1024,2560]{1,0:T(8,128)(2,1)S(1)} %get-tuple-element.196), kind=kOutput, calls=%fused_computation.32 | convolution fusion | flops 5035622400 | bytes 12124160 | tf_op jit(solution)/shard_map/dot_general | solution.py:62
  324.6 7.8 %copy.202 = bf16[2560,960]{1,0:T(8,128)(2,1)} copy(bf16[2560,960]{0,1:T(8,128)(2,1)} %convolution_convert_fusion.5) | data formatting | bytes 9830400 | tf_op jit(solution)/shard_map/convert_element_type | solution.py:218
  336.5 18.2 %multiply_convert_fusion = (bf16[1024,2560]{1,0:T(8,128)(2,1)}, bf16[1024,2560]{1,0:T(8,128)(2,1)}) fusion(f32[1024,2560]{1,0:T(8,128)} %fusion.159, f32[1024,2560]{1,0:T(8,128)} %get-tuple-element.197, bf16[1024,960]{0,1:T(8,128)(2,1)} %fusion.29, bf16[2560,960]{1,0:T(8,128)(2,1)} %bitcast.502), kind=kOutput, calls=%fused_computation.15 | convolution fusion | flops 5067243520 | bytes 38338560 | tf_op jit(solution)/shard_map/dot_general | solution.py:68
  354.7 10.1 %add_convert_fusion = bf16[1024,960]{0,1:T(8,128)(2,1)} fusion(f32[1024,960]{0,1:T(8,128)S(1)} %copy-done.1, bf16[1024,2560]{1,0:T(8,128)(2,1)} %copy-done.86, bf16[2560,960]{1,0:T(8,128)(2,1)} %bitcast.503), kind=kOutput, calls=%fused_computation.62 | convolution fusion | flops 5035130880 | bytes 16056320 | tf_op jit(solution)/shard_map/dot_general | solution.py:58
  368.0 6.1 convolution_convert_fusion.1
  374.1 6.1 convolution_convert_fusion
  380.2 16.8 %collective-permute-done.21 = bf16[8,1,80,960]{3,2,0,1:T(8,128)(2,1)S(1)} collective-permute-done((bf16[8,1,80,960]{3,2,0,1:T(8,128)(2,1)S(1)}, bf16[8,1,80,960]{3,2,0,1:T(8,128)(2,1)S(1)}, u32[]{:S(2)}, u32[]{:S(2)}) %collective-permute-start.21) | collective-permute-done | bytes 1228832 | tf_op jit(solution)/shard_map/ppermute | solution.py:82
  399.3 8.7 %fusion.160 = f32[1024,960]{0,1:T(8,128)} fusion(bf16[1024,2560]{1,0:T(8,128)(2,1)} %get-tuple-element.93, bf16[960,2560]{1,0:T(8,128)(2,1)S(1)} %bitcast.565), kind=kOutput, calls=%fused_computation.293 | convolution fusion | flops 5033164800 | bytes 14090240 | tf_op jit(solution)/shard_map/dot_general | solution.py:68
  411.9 10.0 %multiply_reduce_fusion = (f32[960]{0:T(1024)S(1)}, f32[1024]{0:T(1024)S(1)}, f32[1024,960]{0,1:T(8,128)S(1)}) fusion(f32[1024,960]{0,1:T(8,128)S(1)} %copy-done.1, f32[1024]{0:T(1024)S(1)} %copy-done.54, f32[960]{0:T(1024)S(1)} %copy-done.56, f32[1024,960]{0,1:T(8,128)} %fusion.160, bf16[1024,2560]{1,0:T(8,128)(2,1)} %get-tuple-element.94, ...), kind=kOutput, calls=%fused_computation.56 | convolution fusion | flops 5040044032 | bytes 21970432 | tf_op jit(solution)/shard_map/dot_general | solution.py:68
  429.7 7.3 %fusion.44 = bf16[1024,960]{0,1:T(8,128)(2,1)} fusion(bf16[1024,960]{0,1:T(8,128)(2,1)} %fusion.136, bf16[1024,960]{0,1:T(8,128)(2,1)S(1)} %bitcast.545, s32[1024]{0:T(1024)S(1)} %copy-done.63, s32[1024]{0:T(1024)S(1)} %copy-done.72, s32[1024]{0:T(1024)S(1)} %copy-done.66, s32[1024]{0:T(1024)S(1)} %copy-done.69, pred[1024]{0:T(1024)(128)(4,1)S(1)} %copy-done.78, ...), kind=kOutput, calls=%fused_computation.110 | convolution fusion | flops 4035444736 | bytes 5916672 | tf_op jit(solution)/shard_map/dot_general | solution.py:62
  462.1 27.5 %fusion.4 = bf16[2,5,3,512,512]{3,4,2,1,0:T(8,128)(2,1)} fusion(f32[2,5,3,512,512]{3,4,2,1,0:T(8,128)} %get-tuple-element.193, bf16[2,512,5,3,64]{1,0,4,3,2:T(2,128)(2,1)S(1)} %reshape.1110, bf16[2,512,5,64,1]{1,0,3,2,4:T(2,128)(2,1)S(1)} %bitcast.478), kind=kOutput, calls=%fused_computation.6 | convolution fusion | flops 2044739072 | bytes 49807360 | tf_op jit(solution)/shard_map/sub | solution.py:364
  489.5 10.3 %fusion.86 = bf16[2,512,5,64]{1,3,2,0:T(8,128)(2,1)S(1)} fusion(bf16[2,5,3,512,512]{3,4,2,1,0:T(8,128)(2,1)} %get-tuple-element.82, bf16[2,512,5,3,64]{1,0,4,3,2:T(2,128)(2,1)S(1)} %reshape.1110), kind=kOutput, calls=%fused_computation.154 | convolution fusion | flops 1006960640 | bytes 18350080 | tf_op jit(solution)/shard_map/bgrst,bsgrd->btgd/dot_general | solution.py:362
  512.0 10.3 %multiply_bitcast_fusion = f32[2,512,5,3,64]{1,4,3,2,0:T(8,128)} fusion(bf16[2,5,3,512,512]{3,4,2,1,0:T(8,128)(2,1)} %fusion.4, bf16[2,512,5,64,1]{1,0,3,2,4:T(2,128)(2,1)S(1)} %bitcast.529), kind=kOutput, calls=%fused_computation.57 | convolution fusion | flops 1007616000 | bytes 20316160 | tf_op jit(solution)/shard_map/bgrst,btgd->bsgrd/dot_general | solution.py:368
  522.3 10.3 %fusion.72 = f32[2,512,5,64]{1,3,2,0:T(8,128)S(1)} fusion(bf16[2,5,3,512,512]{3,4,2,1,0:T(8,128)(2,1)} %fusion.4, bf16[2,512,5,3,64]{1,0,4,3,2:T(2,128)(2,1)S(1)} %copy-done.13), kind=kOutput, calls=%fused_computation.127 | convolution fusion | flops 1006960640 | bytes 19005440 | tf_op jit(solution)/shard_map/bgrst,bsgrd->btgd/dot_general | solution.py:372
  555.1 7.7 %collective-permute-done.31 = bf16[4,1,32,2560]{3,2,0,1:T(8,128)(2,1)} collective-permute-done((bf16[4,1,32,2560]{3,2,0,1:T(8,128)(2,1)}, bf16[4,1,32,2560]{3,2,0,1:T(8,128)(2,1)}, u32[]{:S(2)}, u32[]{:S(2)}) %collective-permute-start.31) | collective-permute-done | bytes 655392 | tf_op jit(solution)/shard_map/ppermute | solution.py:82
  575.1 6.3 reshape.1131
  598.4 9.7 %convolution_convert_fusion.6 = bf16[1024,1600]{0,1:T(8,128)(2,1)} fusion(bf16[1024,1600]{0,1:T(8,128)(2,1)} %pad_maximum_fusion.4, bf16[1024,960]{0,1:T(8,128)(2,1)S(1)} %copy-done.20, f32[960]{0:T(1024)S(1)} %copy-done.75, f32[1024]{0:T(1024)S(1)} %copy-done.60, s32[1024]{0:T(1024)S(1)} %copy-done.64, s32[1024]{0:T(1024)S(1)} %copy-done.73, ...), kind=kOutput, calls=%fused_computation.66 | convolution fusion | flops 5382209536 | bytes 8546048 | tf_op jit(solution)/shard_map/dot_general | solution.py:62
  614.3 7.4 %fusion.28 = (f32[960]{0:T(1024)S(1)}, f32[1024]{0:T(1024)S(1)}, f32[1024,960]{0,1:T(8,128)S(1)}) fusion(bf16[1024,960]{0,1:T(8,128)(2,1)S(1)} %copy-done.21, f32[1024]{0:T(1024)S(1)} %copy-done.61, f32[960]{0:T(1024)S(1)} %copy-done.76, bf16[960,1600]{1,0:T(8,128)(2,1)} %copy-done.31, bf16[1024,1600]{0,1:T(8,128)(2,1)} %pad_maximum_fusion.4), kind=kOutput, calls=%fused_computation.55 | convolution fusion | flops 3152607232 | bytes 12262912 | tf_op jit(solution)/shard_map/dot_general | solution.py:68
  645.8 11.9 %collective-permute-done.37 = bf16[8,1,32,1600]{3,2,0,1:T(8,128)(2,1)S(1)} collective-permute-done((bf16[8,1,32,1600]{3,2,0,1:T(8,128)(2,1)S(1)}, bf16[8,1,32,1600]{3,2,0,1:T(8,128)(2,1)S(1)}, u32[]{:S(2)}, u32[]{:S(2)}) %collective-permute-start.37) | collective-permute-done | bytes 819232 | tf_op jit(solution)/shard_map/ppermute | solution.py:82
  658.9 7.2 %collective-permute-done.38 = bf16[4,1,32,1600]{3,2,0,1:T(8,128)(2,1)S(1)} collective-permute-done((bf16[4,1,32,1600]{3,2,0,1:T(8,128)(2,1)S(1)}, bf16[4,1,32,1600]{3,2,0,1:T(8,128)(2,1)S(1)}, u32[]{:S(2)}, u32[]{:S(2)}) %collective-permute-start.38) | collective-permute-done | bytes 409632 | tf_op jit(solution)/shard_map/ppermute | solution.py:82
  668.2 7.2 %collective-permute-done.39 = bf16[1,2,32,1600]{3,2,1,0:T(8,128)(2,1)S(1)} collective-permute-done((bf16[1,2,32,1600]{3,2,1,0:T(8,128)(2,1)S(1)}, bf16[1,2,32,1600]{3,2,1,0:T(8,128)(2,1)S(1)}, u32[]{:S(2)}, u32[]{:S(2)}) %collective-permute-start.39) | collective-permute-done | bytes 204832 | tf_op jit(solution)/shard_map/ppermute | solution.py:82
  (475 shorter events, 290.6 us)
Async XLA Ops:
  12.0 16.9 %collective-permute-start.1 = (bf16[2,32,2560]{2,1,0:T(8,128)(2,1)S(1)}, bf16[2,32,2560]{2,1,0:T(8,128)(2,1)S(1)}, u32[]{:S(2)}, u32[]{:S(2)}) collective-permute-start(bf16[2,32,2560]{2,1,0:T(8,128)(2,1)S(1)} %maximum_bitcast_fusion), channel_id=1, source_target_pairs={{0,16},{1,17},{2,18},{3,19},{4,20},{5,21},{6,22},{7,23},{8,24},{9,... | collective-permute-start | bytes 983048 | tf_op jit(solution)/shard_map/ppermute | solution.py:82
  45.1 29.0 %collective-permute-start.3 = (bf16[8,32,2560]{2,1,0:T(8,128)(2,1)S(1)}, bf16[8,32,2560]{2,1,0:T(8,128)(2,1)}, u32[]{:S(2)}, u32[]{:S(2)}) collective-permute-start(bf16[8,32,2560]{2,1,0:T(8,128)(2,1)S(1)} %bitcast.548), channel_id=1, source_target_pairs={{0,4},{1,5},{2,6},{3,7},{4,0},{5,1},{6,2},{7,3},{8,12},{9,13},{10,... | collective-permute-start | bytes 3932168 | tf_op jit(solution)/shard_map/ppermute | solution.py:82
  110.5 47.5 %collective-permute-start.8 = (bf16[2,32,2560]{2,1,0:T(8,128)(2,1)}, bf16[2,32,2560]{2,1,0:T(8,128)(2,1)}, u32[]{:S(2)}, u32[]{:S(2)}) collective-permute-start(bf16[2,32,2560]{2,1,0:T(8,128)(2,1)} %maximum_bitcast_fusion.1), channel_id=1, source_target_pairs={{0,16},{1,17},{2,18},{3,19},{4,20},{5,21},{6,22},{7,23},{8,24},{9,... | collective-permute-start | bytes 983048 | tf_op jit(solution)/shard_map/ppermute | solution.py:82
  113.9 46.1 %collective-permute-start.9 = (bf16[2,32,2560]{2,1,0:T(8,128)(2,1)}, bf16[2,32,2560]{2,1,0:T(8,128)(2,1)}, u32[]{:S(2)}, u32[]{:S(2)}) collective-permute-start(bf16[2,32,2560]{2,1,0:T(8,128)(2,1)} %maximum_bitcast_fusion.2), channel_id=1, source_target_pairs={{0,16},{1,17},{2,18},{3,19},{4,20},{5,21},{6,22},{7,23},{8,24},{9,... | collective-permute-start | bytes 983048 | tf_op jit(solution)/shard_map/ppermute | solution.py:82
  114.0 42.8 %collective-permute-start.10 = (bf16[2,80,960]{2,1,0:T(8,128)(2,1)}, bf16[2,80,960]{2,1,0:T(8,128)(2,1)}, u32[]{:S(2)}, u32[]{:S(2)}) collective-permute-start(bf16[2,80,960]{2,1,0:T(8,128)(2,1)} %maximum_bitcast_fusion.3), channel_id=1, source_target_pairs={{0,16},{1,17},{2,18},{3,19},{4,20},{5,21},{6,22},{7,23},{8,24},{9,... | collective-permute-start | bytes 921608 | tf_op jit(solution)/shard_map/ppermute | solution.py:82
  162.1 33.2 %collective-permute-start.11 = (bf16[4,32,2560]{2,1,0:T(8,128)(2,1)}, bf16[4,32,2560]{2,1,0:T(8,128)(2,1)}, u32[]{:S(2)}, u32[]{:S(2)}) collective-permute-start(bf16[4,32,2560]{2,1,0:T(8,128)(2,1)} %bitcast.34), channel_id=1, source_target_pairs={{0,4},{1,5},{2,6},{3,7},{4,0},{5,1},{6,2},{7,3},{8,12},{9,13},{10,... | collective-permute-start | bytes 1966088 | tf_op jit(solution)/shard_map/ppermute | solution.py:82
  163.6 29.9 %collective-permute-start.12 = (bf16[4,32,2560]{2,1,0:T(8,128)(2,1)}, bf16[4,32,2560]{2,1,0:T(8,128)(2,1)}, u32[]{:S(2)}, u32[]{:S(2)}) collective-permute-start(bf16[4,32,2560]{2,1,0:T(8,128)(2,1)} %bitcast.37), channel_id=1, source_target_pairs={{0,2},{1,3},{2,0},{3,1},{4,6},{5,7},{6,4},{7,5},{8,10},{9,11},{10,... | collective-permute-start | bytes 1966088 | tf_op jit(solution)/shard_map/ppermute | solution.py:82
  165.1 27.1 %collective-permute-start.13 = (bf16[4,80,960]{2,1,0:T(8,128)(2,1)S(1)}, bf16[4,80,960]{2,1,0:T(8,128)(2,1)}, u32[]{:S(2)}, u32[]{:S(2)}) collective-permute-start(bf16[4,80,960]{2,1,0:T(8,128)(2,1)S(1)} %bitcast.539), channel_id=1, source_target_pairs={{0,4},{1,5},{2,6},{3,7},{4,0},{5,1},{6,2},{7,3},{8,12},{9,13},{10,... | collective-permute-start | bytes 1843208 | tf_op jit(solution)/shard_map/ppermute | solution.py:82
  198.0 31.8 %collective-permute-start.16 = (bf16[8,80,960]{2,1,0:T(8,128)(2,1)S(1)}, bf16[8,80,960]{2,1,0:T(8,128)(2,1)}, u32[]{:S(2)}, u32[]{:S(2)}) collective-permute-start(bf16[8,80,960]{2,1,0:T(8,128)(2,1)S(1)} %bitcast.520), channel_id=1, source_target_pairs={{0,2},{1,3},{2,0},{3,1},{4,6},{5,7},{6,4},{7,5},{8,10},{9,11},{10,... | collective-permute-start | bytes 3686408 | tf_op jit(solution)/shard_map/ppermute | solution.py:82
  202.9 52.1 %collective-permute-start.14 = (bf16[8,32,2560]{2,1,0:T(8,128)(2,1)}, bf16[8,32,2560]{2,1,0:T(8,128)(2,1)S(1)}, u32[]{:S(2)}, u32[]{:S(2)}) collective-permute-start(bf16[8,32,2560]{2,1,0:T(8,128)(2,1)} %bitcast.522), channel_id=1, source_target_pairs={{0,2},{1,3},{2,0},{3,1},{4,6},{5,7},{6,4},{7,5},{8,10},{9,11},{10,... | collective-permute-start | bytes 3932168 | tf_op jit(solution)/shard_map/ppermute | solution.py:82
  203.5 53.4 %collective-permute-start.15 = (bf16[8,32,2560]{2,1,0:T(8,128)(2,1)S(1)}, bf16[8,32,2560]{2,1,0:T(8,128)(2,1)S(1)}, u32[]{:S(2)}, u32[]{:S(2)}) collective-permute-start(bf16[8,32,2560]{2,1,0:T(8,128)(2,1)S(1)} %bitcast.518), channel_id=1, source_target_pairs={{0,4},{1,5},{2,6},{3,7},{4,0},{5,1},{6,2},{7,3},{8,12},{9,13},{10,... | collective-permute-start | bytes 3932168 | tf_op jit(solution)/shard_map/ppermute | solution.py:82
  257.4 19.4 %collective-permute-start.17 = (bf16[16,32,2560]{2,1,0:T(8,128)(2,1)}, bf16[16,32,2560]{2,1,0:T(8,128)(2,1)}, u32[]{:S(2)}, u32[]{:S(2)}) collective-permute-start(bf16[16,32,2560]{2,1,0:T(8,128)(2,1)} %bitcast.60), channel_id=1, source_target_pairs={{0,1},{1,0},{2,3},{3,2},{4,5},{5,4},{6,7},{7,6},{8,9},{9,8},{10,11... | collective-permute-start | bytes 7864328 | tf_op jit(solution)/shard_map/ppermute | solution.py:82
  260.4 34.0 %collective-permute-start.18 = (bf16[16,32,2560]{2,1,0:T(8,128)(2,1)S(1)}, bf16[16,32,2560]{2,1,0:T(8,128)(2,1)S(1)}, u32[]{:S(2)}, u32[]{:S(2)}) collective-permute-start(bf16[16,32,2560]{2,1,0:T(8,128)(2,1)S(1)} %bitcast.487), channel_id=1, source_target_pairs={{0,1},{1,0},{2,3},{3,2},{4,5},{5,4},{6,7},{7,6},{8,9},{9,8},{10,11... | collective-permute-start | bytes 7864328 | tf_op jit(solution)/shard_map/ppermute | solution.py:82
  336.0 28.8 %collective-permute-start.20 = (bf16[16,1,80,960]{3,2,0,1:T(8,128)(2,1)}, bf16[16,1,80,960]{3,2,0,1:T(8,128)(2,1)S(1)}, u32[]{:S(2)}, u32[]{:S(2)}) collective-permute-start(bf16[16,1,80,960]{3,2,0,1:T(8,128)(2,1)} %dynamic-slice_bitcast_fusion.2), channel_id=1, source_target_pairs={{0,1},{1,0},{2,3},{3,2},{4,5},{5,4},{6,7},{7,6},{8,9},{9,8},{10,11... | collective-permute-start | bytes 7372808 | tf_op jit(solution)/shard_map/ppermute | solution.py:82
  366.3 30.8 %collective-permute-start.21 = (bf16[8,1,80,960]{3,2,0,1:T(8,128)(2,1)S(1)}, bf16[8,1,80,960]{3,2,0,1:T(8,128)(2,1)S(1)}, u32[]{:S(2)}, u32[]{:S(2)}) collective-permute-start(bf16[8,1,80,960]{3,2,0,1:T(8,128)(2,1)S(1)} %dynamic-slice_bitcast_fusion.6), channel_id=1, source_target_pairs={{0,2},{1,3},{2,0},{3,1},{4,6},{5,7},{6,4},{7,5},{8,10},{9,11},{10,... | collective-permute-start | bytes 3686408 | tf_op jit(solution)/shard_map/ppermute | solution.py:82
  399.3 28.0 %collective-permute-start.22 = (bf16[16,1,32,2560]{3,2,0,1:T(8,128)(2,1)}, bf16[16,1,32,2560]{3,2,0,1:T(8,128)(2,1)S(1)}, u32[]{:S(2)}, u32[]{:S(2)}) collective-permute-start(bf16[16,1,32,2560]{3,2,0,1:T(8,128)(2,1)} %dynamic-slice_bitcast_fusion.1), channel_id=1, source_target_pairs={{0,1},{1,0},{2,3},{3,2},{4,5},{5,4},{6,7},{7,6},{8,9},{9,8},{10,11... | collective-permute-start | bytes 7864328 | tf_op jit(solution)/shard_map/ppermute | solution.py:82
  409.7 41.5 %collective-permute-start.23 = (bf16[16,1,32,2560]{3,2,0,1:T(8,128)(2,1)}, bf16[16,1,32,2560]{3,2,0,1:T(8,128)(2,1)}, u32[]{:S(2)}, u32[]{:S(2)}) collective-permute-start(bf16[16,1,32,2560]{3,2,0,1:T(8,128)(2,1)} %dynamic-slice_bitcast_fusion), channel_id=1, source_target_pairs={{0,1},{1,0},{2,3},{3,2},{4,5},{5,4},{6,7},{7,6},{8,9},{9,8},{10,11... | collective-permute-start | bytes 7864328 | tf_op jit(solution)/shard_map/ppermute | solution.py:82
  410.3 16.7 %collective-permute-start.24 = (bf16[4,1,80,960]{3,2,0,1:T(8,128)(2,1)S(1)}, bf16[4,1,80,960]{3,2,0,1:T(8,128)(2,1)S(1)}, u32[]{:S(2)}, u32[]{:S(2)}) collective-permute-start(bf16[4,1,80,960]{3,2,0,1:T(8,128)(2,1)S(1)} %dynamic-slice_bitcast_fusion.11), channel_id=1, source_target_pairs={{0,4},{1,5},{2,6},{3,7},{4,0},{5,1},{6,2},{7,3},{8,12},{9,13},{10,... | collective-permute-start | bytes 1843208 | tf_op jit(solution)/shard_map/ppermute | solution.py:82
  455.9 47.4 %collective-permute-start.25 = (bf16[16,1,32,960]{3,2,0,1:T(8,128)(2,1)}, bf16[16,1,32,960]{3,2,0,1:T(8,128)(2,1)}, u32[]{:S(2)}, u32[]{:S(2)}) collective-permute-start(bf16[16,1,32,960]{3,2,0,1:T(8,128)(2,1)} %dynamic-slice_bitcast_fusion.7), channel_id=1, source_target_pairs={{0,1},{1,0},{2,3},{3,2},{4,5},{5,4},{6,7},{7,6},{8,9},{9,8},{10,11... | collective-permute-start | bytes 2949128 | tf_op jit(solution)/shard_map/ppermute | solution.py:82
  457.1 49.3 %collective-permute-start.26 = (bf16[4,2,32,2560]{3,2,1,0:T(8,128)(2,1)}, bf16[4,2,32,2560]{3,2,1,0:T(8,128)(2,1)}, u32[]{:S(2)}, u32[]{:S(2)}) collective-permute-start(bf16[4,2,32,2560]{3,2,1,0:T(8,128)(2,1)} %dynamic-slice_bitcast_fusion.5), channel_id=1, source_target_pairs={{0,4},{1,5},{2,6},{3,7},{4,0},{5,1},{6,2},{7,3},{8,12},{9,13},{10,... | collective-permute-start | bytes 3932168 | tf_op jit(solution)/shard_map/ppermute | solution.py:82
  459.8 49.4 %collective-permute-start.27 = (bf16[8,1,32,2560]{3,2,0,1:T(8,128)(2,1)}, bf16[8,1,32,2560]{3,2,0,1:T(8,128)(2,1)}, u32[]{:S(2)}, u32[]{:S(2)}) collective-permute-start(bf16[8,1,32,2560]{3,2,0,1:T(8,128)(2,1)} %dynamic-slice_bitcast_fusion.4), channel_id=1, source_target_pairs={{0,2},{1,3},{2,0},{3,1},{4,6},{5,7},{6,4},{7,5},{8,10},{9,11},{10,... | collective-permute-start | bytes 3932168 | tf_op jit(solution)/shard_map/ppermute | solution.py:82
  462.1 39.5 %collective-permute-start.28 = (bf16[1,2,80,960]{3,2,1,0:T(8,128)(2,1)}, bf16[1,2,80,960]{3,2,1,0:T(8,128)(2,1)}, u32[]{:S(2)}, u32[]{:S(2)}) collective-permute-start(bf16[1,2,80,960]{3,2,1,0:T(8,128)(2,1)} %dynamic-slice_bitcast_fusion.16), channel_id=1, source_target_pairs={{0,16},{1,17},{2,18},{3,19},{4,20},{5,21},{6,22},{7,23},{8,24},{9,... | collective-permute-start | bytes 921608 | tf_op jit(solution)/shard_map/ppermute | solution.py:82
  537.2 16.6 %collective-permute-start.30 = (bf16[4,1,32,2560]{3,2,0,1:T(8,128)(2,1)}, bf16[4,1,32,2560]{3,2,0,1:T(8,128)(2,1)}, u32[]{:S(2)}, u32[]{:S(2)}) collective-permute-start(bf16[4,1,32,2560]{3,2,0,1:T(8,128)(2,1)} %dynamic-slice_bitcast_fusion.10), channel_id=1, source_target_pairs={{0,2},{1,3},{2,0},{3,1},{4,6},{5,7},{6,4},{7,5},{8,10},{9,11},{10,... | collective-permute-start | bytes 1966088 | tf_op jit(solution)/shard_map/ppermute | solution.py:82
  546.5 16.3 %collective-permute-start.31 = (bf16[4,1,32,2560]{3,2,0,1:T(8,128)(2,1)}, bf16[4,1,32,2560]{3,2,0,1:T(8,128)(2,1)}, u32[]{:S(2)}, u32[]{:S(2)}) collective-permute-start(bf16[4,1,32,2560]{3,2,0,1:T(8,128)(2,1)} %dynamic-slice_bitcast_fusion.9), channel_id=1, source_target_pairs={{0,4},{1,5},{2,6},{3,7},{4,0},{5,1},{6,2},{7,3},{8,12},{9,13},{10,... | collective-permute-start | bytes 1966088 | tf_op jit(solution)/shard_map/ppermute | solution.py:82
  564.1 23.3 %collective-permute-start.32 = (bf16[4,1,32,960]{3,2,0,1:T(8,128)(2,1)S(1)}, bf16[4,1,32,960]{3,2,0,1:T(8,128)(2,1)}, u32[]{:S(2)}, u32[]{:S(2)}) collective-permute-start(bf16[4,1,32,960]{3,2,0,1:T(8,128)(2,1)S(1)} %dynamic-slice_bitcast_fusion.17), channel_id=1, source_target_pairs={{0,2},{1,3},{2,0},{3,1},{4,6},{5,7},{6,4},{7,5},{8,10},{9,11},{10,... | collective-permute-start | bytes 737288 | tf_op jit(solution)/shard_map/ppermute | solution.py:82
  565.9 25.9 %collective-permute-start.33 = (bf16[1,2,32,2560]{3,2,1,0:T(8,128)(2,1)}, bf16[1,2,32,2560]{3,2,1,0:T(8,128)(2,1)}, u32[]{:S(2)}, u32[]{:S(2)}) collective-permute-start(bf16[1,2,32,2560]{3,2,1,0:T(8,128)(2,1)} %dynamic-slice_bitcast_fusion.15), channel_id=1, source_target_pairs={{0,16},{1,17},{2,18},{3,19},{4,20},{5,21},{6,22},{7,23},{8,24},{9,... | collective-permute-start | bytes 983048 | tf_op jit(solution)/shard_map/ppermute | solution.py:82
  568.8 27.0 %collective-permute-start.34 = (bf16[1,2,32,2560]{3,2,1,0:T(8,128)(2,1)}, bf16[1,2,32,2560]{3,2,1,0:T(8,128)(2,1)}, u32[]{:S(2)}, u32[]{:S(2)}) collective-permute-start(bf16[1,2,32,2560]{3,2,1,0:T(8,128)(2,1)} %dynamic-slice_bitcast_fusion.14), channel_id=1, source_target_pairs={{0,16},{1,17},{2,18},{3,19},{4,20},{5,21},{6,22},{7,23},{8,24},{9,... | collective-permute-start | bytes 983048 | tf_op jit(solution)/shard_map/ppermute | solution.py:82
  613.9 25.2 %collective-permute-start.36 = (bf16[16,1,32,1600]{3,2,0,1:T(8,128)(2,1)S(1)}, bf16[16,1,32,1600]{3,2,0,1:T(8,128)(2,1)S(1)}, u32[]{:S(2)}, u32[]{:S(2)}) collective-permute-start(bf16[16,1,32,1600]{3,2,0,1:T(8,128)(2,1)S(1)} %dynamic-slice_bitcast_fusion.3), channel_id=1, source_target_pairs={{0,1},{1,0},{2,3},{3,2},{4,5},{5,4},{6,7},{7,6},{8,9},{9,8},{10,11... | collective-permute-start | bytes 4915208 | tf_op jit(solution)/shard_map/ppermute | solution.py:82
  622.0 36.9 %collective-permute-start.42 = (bf16[1,1,32,2560]{3,2,1,0:T(8,128)(2,1)S(1)}, bf16[1,1,32,2560]{3,2,1,0:T(8,128)(2,1)S(1)}, u32[]{:S(2)}, u32[]{:S(2)}) collective-permute-start(bf16[1,1,32,2560]{3,2,1,0:T(8,128)(2,1)S(1)} %get-tuple-element.171), channel_id=1, source_target_pairs={{0,8},{1,9},{2,10},{3,11},{4,12},{5,13},{6,14},{7,15},{8,0},{9,1},... | collective-permute-start | bytes 491528 | tf_op jit(solution)/shard_map/ppermute | solution.py:82
  627.1 39.5 %collective-permute-start.43 = (bf16[1,1,32,2560]{3,2,1,0:T(8,128)(2,1)S(1)}, bf16[1,1,32,2560]{3,2,1,0:T(8,128)(2,1)S(1)}, u32[]{:S(2)}, u32[]{:S(2)}) collective-permute-start(bf16[1,1,32,2560]{3,2,1,0:T(8,128)(2,1)S(1)} %get-tuple-element.169), channel_id=1, source_target_pairs={{0,8},{1,9},{2,10},{3,11},{4,12},{5,13},{6,14},{7,15},{8,0},{9,1},... | collective-permute-start | bytes 491528 | tf_op jit(solution)/shard_map/ppermute | solution.py:82
  633.7 41.9 %collective-permute-start.41 = (bf16[1,1,32,960]{3,2,1,0:T(8,128)(2,1)S(1)}, bf16[1,1,32,960]{3,2,1,0:T(8,128)(2,1)}, u32[]{:S(2)}, u32[]{:S(2)}) collective-permute-start(bf16[1,1,32,960]{3,2,1,0:T(8,128)(2,1)S(1)} %get-tuple-element.183), channel_id=1, source_target_pairs={{0,8},{1,9},{2,10},{3,11},{4,12},{5,13},{6,14},{7,15},{8,0},{9,1},... | collective-permute-start | bytes 184328 | tf_op jit(solution)/shard_map/ppermute | solution.py:82
  639.7 18.0 %collective-permute-start.37 = (bf16[8,1,32,1600]{3,2,0,1:T(8,128)(2,1)S(1)}, bf16[8,1,32,1600]{3,2,0,1:T(8,128)(2,1)S(1)}, u32[]{:S(2)}, u32[]{:S(2)}) collective-permute-start(bf16[8,1,32,1600]{3,2,0,1:T(8,128)(2,1)S(1)} %dynamic-slice_bitcast_fusion.8), channel_id=1, source_target_pairs={{0,2},{1,3},{2,0},{3,1},{4,6},{5,7},{6,4},{7,5},{8,10},{9,11},{10,... | collective-permute-start | bytes 2457608 | tf_op jit(solution)/shard_map/ppermute | solution.py:82
  (115 other events, 1960.0 us)
